TPU v7x, 32 devices: a whole 2x2x4 slice. The times are simulated.
32 devices in a mesh: parts: 2 (over y), expert: 4 (over x, core), seq: 4 (over z).
Axes of the slice: x: 2, y: 2, z: 4, core: 2. Of those that a mesh axis runs over, the one named last changes fastest.
Arguments:
- tokens: bfloat16 [1024, 5120], P(('parts', 'expert'), 'seq'), parts along dimension 0, may hold values from -6 to 6
- expert_ids: int32 [1024, 6], P(('parts', 'expert')), parts along dimension 0, may hold values from 0 to 7, as said below
- gates: float32 [1024, 6], P(('parts', 'expert')), parts along dimension 0, may hold values from 0.1 to 2
- hot_list: int32 [4], P('parts'), parts along dimension 0, may hold values from 0 to 7, as said below
- w_gate: bfloat16 [8, 5120, 1536], P('expert', None, 'seq'), may hold values from -0.078125 to 0.078125
- w_up: bfloat16 [8, 5120, 1536], P('expert', None, 'seq'), may hold values from -0.078125 to 0.078125
- w_down: bfloat16 [8, 1536, 5120], P('expert', 'seq'), may hold values from -0.15625 to 0.15625
Outputs:
- moved: bfloat16 [1024, 5120], P(('parts', 'expert'), 'seq'), parts along dimension 0
There are 2 independent parts, one for each index of `parts`. A program takes and returns all parts, laid end to end along the dimension named above; an argument that names none is the same for every part. Nothing has to cross between parts.
Inputs may be any that keep to these rules, and one draw needn't show every extreme that they name: `expert_ids`: each row names 6 different experts. `hot_list`: 2 different experts.
All inputs are finite; a program needn't handle non-finite values.
Results may differ from a plain program's by a relative error of at most 0.0058.
Values may be sent and summed in bfloat16 or wider, within the bound.
No kernel may reach another device: no remote copies, remote signals or barrier semaphores. Data moves between devices by JAX's collectives and lax.ppermute only.
A program may use at most 192 MiB of HBM per device.

v0:
```python
import jax
import jax.numpy as jnp
from jax import lax
from jax.sharding import PartitionSpec as P


def broadcast(value, axis, source):
    kept = jnp.where(lax.axis_index(axis) == source, value, 0).astype(value.dtype)
    return lax.psum(kept, axis)


def expert_slice(rows, gate_part, up_part, down_part):
    gate_value = jnp.dot(rows, gate_part, preferred_element_type=jnp.float32)
    up_value = jnp.dot(rows, up_part, preferred_element_type=jnp.float32)
    hidden = (jax.nn.silu(gate_value) * up_value).astype(jnp.bfloat16)
    return jnp.dot(hidden, down_part, preferred_element_type=jnp.float32).astype(jnp.bfloat16)


def body(tokens, expert_ids, gates, hot_list, w_gate, w_up, w_down):
    owner_count = lax.axis_size("expert")
    local_count = w_gate.shape[0]
    expert_count = local_count * owner_count
    row_count = expert_ids.shape[0]
    pick_count = expert_ids.shape[1]
    feature_count = w_down.shape[2]
    capacity = 3 * row_count * pick_count // (4 * expert_count)
    whole = lax.all_gather(tokens, "seq", axis=1, tiled=True)
    flat_ids = expert_ids.reshape(-1)
    flat_weights = gates.reshape(-1)
    flat_rows = jnp.arange(row_count * pick_count, dtype=jnp.int32) // pick_count
    onehot = (flat_ids[:, None] == jnp.arange(expert_count, dtype=jnp.int32)[None, :]).astype(
        jnp.int32
    )
    earlier = jnp.cumsum(onehot, axis=0) - onehot
    slot_index = jnp.sum(earlier * onehot, axis=1)
    hot_route = jnp.any(flat_ids[:, None] == hot_list[None, :], axis=1)
    kept_cold = jnp.logical_and(jnp.logical_not(hot_route), slot_index < capacity)
    buffer_size = expert_count * capacity
    buffer_place = jnp.where(kept_cold, flat_ids * capacity + slot_index, buffer_size)
    slot_rows = jnp.zeros((buffer_size,), jnp.int32).at[buffer_place].set(flat_rows, mode="drop")
    outgoing = whole[slot_rows].reshape(owner_count, local_count * capacity, feature_count)
    incoming = lax.all_to_all(outgoing, "expert", split_axis=0, concat_axis=0, tiled=True)
    blocks = incoming.reshape(owner_count, local_count, capacity, feature_count)
    results = []
    for local_index in range(local_count):
        rows = blocks[:, local_index].reshape(owner_count * capacity, feature_count)
        output = expert_slice(rows, w_gate[local_index], w_up[local_index], w_down[local_index])
        results.append(output.reshape(owner_count, 1, capacity, feature_count))
    partial_value = jnp.concatenate(results, axis=1).reshape(
        owner_count, local_count * capacity, feature_count
    )
    hot_total = jnp.zeros((row_count, feature_count), jnp.float32)
    for hot_index in range(hot_list.shape[0]):
        chosen = hot_list[hot_index]
        local_pick = chosen % local_count
        owner_pick = chosen // local_count
        pieces = (
            lax.dynamic_index_in_dim(w_gate, local_pick, 0, False),
            lax.dynamic_index_in_dim(w_up, local_pick, 0, False),
            lax.dynamic_index_in_dim(w_down, local_pick, 0, False),
        )
        received = (
            broadcast(pieces[0], "expert", owner_pick),
            broadcast(pieces[1], "expert", owner_pick),
            broadcast(pieces[2], "expert", owner_pick),
        )
        hot_out = lax.optimization_barrier(
            expert_slice(whole, received[0], received[1], received[2])
        )
        weight = jnp.sum(jnp.where(expert_ids == chosen, gates, 0.0), axis=1)
        hot_total = hot_total + weight[:, None] * hot_out.astype(jnp.float32)
    route_place = jnp.minimum(buffer_place, buffer_size - 1).reshape(row_count, pick_count)
    route_weight = jnp.where(kept_cold, flat_weights, 0.0).reshape(row_count, pick_count)
    returned = lax.all_to_all(
        partial_value, "expert", split_axis=0, concat_axis=0, tiled=True
    ).reshape(buffer_size, feature_count)
    combined = hot_total
    for route_index in range(pick_count):
        picked = returned[route_place[:, route_index]].astype(jnp.float32)
        combined = combined + route_weight[:, route_index : route_index + 1] * picked
    moved = lax.psum_scatter(combined, "seq", scatter_dimension=1, tiled=True)
    return moved.astype(jnp.bfloat16)


def solution(mesh):
    placed = (
        P(("parts", "expert"), "seq"),
        P(("parts", "expert"), None),
        P(("parts", "expert"), None),
        P("parts"),
        P("expert", None, "seq"),
        P("expert", None, "seq"),
        P("expert", "seq", None),
    )
    return jax.shard_map(
        body, mesh=mesh, in_specs=placed, out_specs=P(("parts", "expert"), "seq"), check_vma=False
    )
```

profile of v0, /device:TPU:0, one launch (start us, length us, event | category | flops | bytes accessed | tf_op | source)
XLA Modules:
  0.0 677.0 jit_solution(1691484590291072246)
XLA Ops:
  17.1 28.1 %all-gather.2.cloned.1.call-done = bf16[128,5120]{1,0:T(8,128)(2,1)} async-done(((bf16[128,1280]{1,0:T(8,128)(2,1)}), bf16[128,5120]{1,0:T(8,128)(2,1)}) %all-gather.2.cloned.1.call-update) | async-done | bytes 1310736 | tf_op jit(solution)/shard_map/all_gather | solution.py:27
  45.2 15.5 %gather_fusion = bf16[576,5120]{1,0:T(8,128)(2,1)} fusion(bf16[128,5120]{1,0:T(8,128)(2,1)} %all-gather.2.cloned.1.call-done, s32[1024]{0:T(1024)S(1)} %pad_clamp_fusion.6), kind=kCustom, calls=%fused_computation | custom fusion | bytes 11798784 | tf_op jit(solution)/shard_map/gather | solution.py:41
  60.7 5.3 all-to-all-start
  72.0 7.0 %select_bitcast_fusion.3 = (bf16[384,5120]{1,0:T(8,128)(2,1)}, bf16[384,5120]{1,0:T(8,128)(2,1)}) fusion(bf16[2,384,5120]{2,1,0:T(8,128)(2,1)} %param.13, s32[]{:T(128)S(6)} %select_n.156, pred[]{:T(512)S(6)} %eq.65, s32[]{:T(128)S(6)} %select_n.168, pred[]{:T(512)S(6)} %eq.68), kind=kLoop, calls=%fused_computation.32 | loop fusion | flops 3932160 | bytes 15728650 | tf_op jit(solution)/shard_map/jit(_where)/select_n | solution.py:8
  79.0 11.4 %select_bitcast_fusion.4 = (bf16[5120,384]{1,0:T(8,128)(2,1)}, bf16[5120,384]{1,0:T(8,128)(2,1)}, bf16[5120,384]{1,0:T(8,128)(2,1)}, bf16[5120,384]{1,0:T(8,128)(2,1)}) fusion(bf16[2,5120,384]{2,1,0:T(8,128)(2,1)} %param.12, s32[]{:T(128)S(6)} %select_n.156, pred[]{:T(512)S(6)} %eq.65, s32[]{:T(128)S(6)} %select_n.168, pred[]{:T(512)S(6)} %eq.68, ...), kind=kLoop, calls=%fused_computation.33 | loop fusion | flops 7864320 | bytes 31457290 | tf_op jit(solution)/shard_map/jit(_where)/select_n | solution.py:8
  90.4 77.5 %all-to-all-done = bf16[4,144,5120]{2,1,0:T(8,128)(2,1)} async-done(((bf16[4,144,5120]{2,1,0:T(8,128)(2,1)}), bf16[4,144,5120]{2,1,0:T(8,128)(2,1)}, u32[]{:S(2)}, u32[]{:S(2)}) %all-to-all-start) | async-done | bytes 5898272 | tf_op jit(solution)/shard_map/all_to_all | solution.py:42
  171.3 5.8 fusion.8
  177.1 3.8 fusion.3
  180.8 9.6 %convolution_convert_fusion.1 = bf16[288,5120]{1,0:T(8,128)(2,1)} fusion(bf16[2,384,5120]{2,1,0:T(8,128)(2,1)} %param.13, bf16[288,5120]{1,0:T(8,128)(2,1)} %bitcast.129, bf16[2,5120,384]{2,1,0:T(8,128)(2,1)} %param.12, f32[288,384]{1,0:T(8,128)} %fusion.8), kind=kOutput, calls=%fused_computation.9 | convolution fusion | flops 2267062272 | bytes 14204928 | tf_op jit(solution)/shard_map/dot_general | solution.py:16
  190.4 8.7 %convolution_convert_fusion = bf16[288,5120]{1,0:T(8,128)(2,1)} fusion(bf16[2,384,5120]{2,1,0:T(8,128)(2,1)} %param.13, bf16[288,5120]{1,0:T(8,128)(2,1)S(1)} %bitcast.127, bf16[2,5120,384]{2,1,0:T(8,128)(2,1)} %param.12, f32[288,384]{1,0:T(8,128)S(1)} %fusion.3), kind=kOutput, calls=%fused_computation.8 | convolution fusion | flops 2267062272 | bytes 14204928 | tf_op jit(solution)/shard_map/dot_general | solution.py:16
  199.1 5.8 pad_maximum_fusion
  205.0 5.3 all-to-all-start.1
  212.0 128.4 %all-to-all-done.1 = bf16[4,144,5120]{2,1,0:T(8,128)(2,1)} async-done(((bf16[4,144,5120]{2,1,0:T(8,128)(2,1)}), bf16[4,144,5120]{2,1,0:T(8,128)(2,1)}, u32[]{:S(2)}, u32[]{:S(2)}) %all-to-all-start.1) | async-done | bytes 5898272 | tf_op jit(solution)/shard_map/all_to_all | solution.py:74
  340.3 6.0 gather_fusion.1
  346.4 7.3 %gather_fusion.2 = bf16[128,5120]{1,0:T(8,128)(2,1)} fusion(bf16[576,5120]{1,0:T(8,128)(2,1)} %bitcast.31, s32[1024]{0:T(1024)S(1)} %get-tuple-element.42), kind=kCustom, calls=%fused_computation.2 | custom fusion | bytes 2621952 | tf_op jit(solution)/shard_map/gather | solution.py:79
  353.7 7.1 %gather_fusion.3 = bf16[128,5120]{1,0:T(8,128)(2,1)} fusion(bf16[576,5120]{1,0:T(8,128)(2,1)} %bitcast.31, s32[1024]{0:T(1024)S(1)} %get-tuple-element.41), kind=kCustom, calls=%fused_computation.3 | custom fusion | bytes 2621952 | tf_op jit(solution)/shard_map/gather | solution.py:79
  360.8 7.5 %gather_fusion.4 = bf16[128,5120]{1,0:T(8,128)(2,1)} fusion(bf16[576,5120]{1,0:T(8,128)(2,1)} %bitcast.31, s32[1024]{0:T(1024)S(1)} %get-tuple-element.40), kind=kCustom, calls=%fused_computation.4 | custom fusion | bytes 2621952 | tf_op jit(solution)/shard_map/gather | solution.py:79
  368.3 7.1 %gather_fusion.5 = bf16[128,5120]{1,0:T(8,128)(2,1)} fusion(bf16[576,5120]{1,0:T(8,128)(2,1)} %bitcast.31, s32[1024]{0:T(1024)S(1)} %get-tuple-element.39), kind=kCustom, calls=%fused_computation.5 | custom fusion | bytes 2621952 | tf_op jit(solution)/shard_map/gather | solution.py:79
  375.4 7.4 %gather_fusion.6 = bf16[128,5120]{1,0:T(8,128)(2,1)} fusion(bf16[576,5120]{1,0:T(8,128)(2,1)} %bitcast.31, s32[1024]{0:T(1024)S(1)} %get-tuple-element.38), kind=kCustom, calls=%fused_computation.6 | custom fusion | bytes 2621952 | tf_op jit(solution)/shard_map/gather | solution.py:79
  382.8 203.9 %all-reduce.3.cloned.1.call-done = (bf16[384,5120]{1,0:T(8,128)(2,1)}, bf16[5120,384]{1,0:T(8,128)(2,1)}, bf16[5120,384]{1,0:T(8,128)(2,1)}, bf16[384,5120]{1,0:...) async-done(((bf16[384,5120]{1,0:T(8,128)(2,1)}, bf16[5120,384]{1,0:T(8,128)(2,1)}, bf16[5120,384]{1,0:T(8,128)(2,1)}, bf16[384,5120]{1,0:T(8,128)(2,1)}, ...) | async-done | bytes 23592976 | tf_op jit(solution)/shard_map/psum | solution.py:9
  590.0 7.7 %convolution_convert_fusion.3 = bf16[128,5120]{1,0:T(8,128)(2,1)} fusion(bf16[384,5120]{1,0:T(8,128)(2,1)} %get-tuple-element.10, bf16[5120,384]{1,0:T(8,128)(2,1)} %get-tuple-element.11, bf16[128,5120]{1,0:T(8,128)(2,1)S(1)} %copy-done, f32[128,384]{0,1:T(8,128)S(1)} %convolution_bitcast_fusion.3), kind=kOutput, calls=%fused_computation.11 | convolution fusion | flops 1007583232 | bytes 10682368 | tf_op jit(solution)/shard_map/dot_general | solution.py:16
  601.0 7.9 %convolution_convert_fusion.2 = bf16[128,5120]{1,0:T(8,128)(2,1)} fusion(bf16[384,5120]{1,0:T(8,128)(2,1)} %get-tuple-element.7, bf16[5120,384]{1,0:T(8,128)(2,1)} %get-tuple-element.8, bf16[128,5120]{1,0:T(8,128)(2,1)S(1)} %copy-done, f32[128,384]{0,1:T(8,128)S(1)} %convolution_bitcast_fusion.1), kind=kOutput, calls=%fused_computation.10 | convolution fusion | flops 1007583232 | bytes 10682368 | tf_op jit(solution)/shard_map/dot_general | solution.py:16
  608.9 6.1 multiply_add_fusion
  615.0 52.5 %reduce-scatter.2.cloned.1.call-done = f32[128,1280]{1,0:T(8,128)} async-done(((f32[128,5120]{1,0:T(8,128)}), f32[128,1280]{1,0:T(8,128)}) %reduce-scatter.2.cloned.1.call-update) | async-done | bytes 655376 | tf_op jit(solution)/shard_map/reduce_scatter | solution.py:81
  (51 shorter events, 23.9 us)
Async XLA Ops:
  7.4 37.8 %all-gather.2.cloned.1.call-start = ((), (), s32[]{:S(2)}) async-start(), calls=%async_computation.3 | async-start | bytes 1638400 | tf_op jit(solution)/shard_map/all_gather | solution.py:27
  60.7 5.5 copy-start.3
  60.7 107.3 %all-to-all-start = ((bf16[4,144,5120]{2,1,0:T(8,128)(2,1)}), bf16[4,144,5120]{2,1,0:T(8,128)(2,1)}, u32[]{:S(2)}, u32[]{:S(2)}) async-start(bf16[4,144,5120]{2,1,0:T(8,128)(2,1)} %bitcast.124), calls=%async_computation | async-start | bytes 11796480 | tf_op jit(solution)/shard_map/all_to_all | solution.py:42
  66.0 520.6 %all-reduce.3.cloned.1.call-start = ((), (), s32[]{:S(2)}) async-start(), calls=%async_computation.5 | async-start | bytes 47185920 | tf_op jit(solution)/shard_map/psum | solution.py:9
  171.3 5.8 copy-start.1
  205.0 5.7 copy-start.2
  205.0 5.7 copy-start.4
  205.0 135.4 %all-to-all-start.1 = ((bf16[4,144,5120]{2,1,0:T(8,128)(2,1)}), bf16[4,144,5120]{2,1,0:T(8,128)(2,1)}, u32[]{:S(2)}, u32[]{:S(2)}) async-start(bf16[4,144,5120]{2,1,0:T(8,128)(2,1)} %bitcast.125), calls=%async_computation.1 | async-start | bytes 11796480 | tf_op jit(solution)/shard_map/all_to_all | solution.py:74
  210.3 457.2 %reduce-scatter.2.cloned.1.call-start = ((), (), s32[]{:S(2)}) async-start(), calls=%async_computation.4 | async-start | bytes 3276800 | tf_op jit(solution)/shard_map/reduce_scatter | solution.py:81
  375.4 211.3 %copy-start = (bf16[128,5120]{1,0:T(8,128)(2,1)S(1)}, bf16[128,5120]{1,0:T(8,128)(2,1)}, u32[]{:S(2)}) copy-start(bf16[128,5120]{1,0:T(8,128)(2,1)} %all-gather.2.cloned.1.call-done) | copy-start | bytes 3932164
Sparse Core Ops, SparseCore 0:
  9.8 35.3 all-gather.1
  615.2 52.3 reduce-scatter.1
Sparse Core Ops, SparseCore 1:
  90.5 496.1 all-reduce.2
where the time goes:
time: 683 us; the launch traced here: 677 us
  waiting for transfers between devices  491 us (72%)
  local copies, waits for them, and re-layouts  67.3 us (10%)
  matrix products  50.1 us (7%)
  other arithmetic  36.9 us (5%)
  between operations  20.4 us (3%)
  starting transfers between devices  11.1 us (2%)
    psum x1, waiting for transfers between devices, broadcast(): return lax.psum(kept, axis)  204 us
    all_to_all x1, waiting for transfers between devices, body(): lax.all_to_all(partial_value, 'expert', split_axis=0, concat_axis=0, tile...  128 us
    all_to_all x1, waiting for transfers between devices, body(): lax.all_to_all(outgoing, 'expert', split_axis=0, concat_axis=0, tiled=True)  77.5 us
    reduce_scatter x1, waiting for transfers between devices, body(): moved = lax.psum_scatter(combined, 'seq', scatter_dimension=1, tiled=True)  52.5 us
    gather x6, local copies, waits for them, and re-layouts, body(): picked = returned[route_place[:, route_index]].astype(jnp.float32)  42.4 us
    dot_general x4, matrix products, expert_slice(): jnp.dot(hidden, down_part, preferred_element_type=jnp.float32)  33.9 us
    all_gather x1, waiting for transfers between devices, body(): whole = lax.all_gather(tokens, 'seq', axis=1, tiled=True)  28.1 us
    select_n x2, other arithmetic, broadcast(): jnp.where(lax.axis_index(axis) == source, value, 0).astype(value.dtype)  18.4 us
  transfers between devices with their start and end apart: 5, of which 5 were waited for; matrix products, arithmetic and copies ran while one was open for 16% of the time, Pallas kernels for 0%

commit v1 on v0

v1 whole, which is shorter than its diff:
```python
import functools

import jax
import jax.numpy as jnp
from jax import lax
from jax.experimental import pallas as pl
from jax.experimental.pallas import tpu as pltpu
from jax.sharding import PartitionSpec as P

VMEM_LIMIT = 60 * 1024 * 1024


def dot(a, b):
    return jnp.dot(a, b, preferred_element_type=jnp.float32)


def gate_up_kernel(first, at_ref, *refs):
    near_ref, far_ref, gate_ref, up_ref = refs[:4]
    out_ref = refs[-1]
    half, width = near_ref.shape[0], gate_ref.shape[2]
    for side, rows_ref in enumerate((near_ref, far_ref)):
        rows = slice(side * half, (side + 1) * half)
        for place, part_ref in enumerate((gate_ref, up_ref)):
            value = dot(rows_ref[...], part_ref[0])
            if not first:
                value = value + refs[4][0, place, rows]
            out_ref[0, place, rows] = value


def hidden_kernel(at_ref, near_ref, far_ref, gate_ref, up_ref, total_ref, weight_ref, out_ref):
    half, width = near_ref.shape[0], gate_ref.shape[2]
    for local_index in range(weight_ref.shape[1]):

        @pl.when(pl.program_id(0) == local_index)
        def _():
            for side, rows_ref in enumerate((near_ref, far_ref)):
                rows = slice(side * half, (side + 1) * half)
                gate_value = dot(rows_ref[...], gate_ref[0]) + total_ref[0, 0, rows]
                up_value = dot(rows_ref[...], up_ref[0]) + total_ref[0, 1, rows]
                value = gate_value / (1.0 + jnp.exp(-gate_value)) * up_value
                value = value * weight_ref[rows, local_index : local_index + 1]
                columns = slice(local_index * width, (local_index + 1) * width)
                out_ref[rows, columns] = value.astype(jnp.bfloat16)


def down_kernel(at_ref, hidden_ref, down_ref, keep_ref, send_ref):
    half = keep_ref.shape[0]
    send_ref[...] = dot(hidden_ref[half:], down_ref[...]).astype(jnp.bfloat16)
    keep_ref[...] = dot(hidden_ref[:half], down_ref[...])


def gate_up(at, near, far, w_gate, w_up, total):
    local_count, _, width = w_gate.shape
    half, depth = near.shape
    rows_spec = pl.BlockSpec((half, depth), lambda i, at: (0, 0))
    part_spec = pl.BlockSpec((1, depth, width), lambda i, at: (i, at[0], 0))
    total_spec = pl.BlockSpec((1, 2, 2 * half, width), lambda i, at: (i, 0, 0, 0))
    first = total is None
    flops = 2 * local_count * 2 * half * depth * 2 * width
    return pl.pallas_call(
        functools.partial(gate_up_kernel, first),
        out_shape=jax.ShapeDtypeStruct((local_count, 2, 2 * half, width), jnp.float32),
        grid_spec=pltpu.PrefetchScalarGridSpec(
            num_scalar_prefetch=1,
            grid=(local_count,),
            in_specs=[rows_spec, rows_spec, part_spec, part_spec] + [total_spec] * (not first),
            out_specs=total_spec,
        ),
        compiler_params=pltpu.CompilerParams(vmem_limit_bytes=VMEM_LIMIT),
        cost_estimate=pl.CostEstimate(flops=flops, bytes_accessed=8 << 20, transcendentals=0),
    )(at, near, far, w_gate, w_up, *([] if first else [total]))


def hidden(at, near, far, w_gate, w_up, total, weight):
    local_count, _, width = w_gate.shape
    half, depth = near.shape
    rows_spec = pl.BlockSpec((half, depth), lambda i, at: (0, 0))
    part_spec = pl.BlockSpec((1, depth, width), lambda i, at: (i, at[0], 0))
    total_spec = pl.BlockSpec((1, 2, 2 * half, width), lambda i, at: (i, 0, 0, 0))
    flops = 2 * local_count * 2 * half * depth * 2 * width
    return pl.pallas_call(
        hidden_kernel,
        out_shape=jax.ShapeDtypeStruct((2 * half, local_count * width), jnp.bfloat16),
        grid_spec=pltpu.PrefetchScalarGridSpec(
            num_scalar_prefetch=1,
            grid=(local_count,),
            in_specs=[
                rows_spec,
                rows_spec,
                part_spec,
                part_spec,
                total_spec,
                pl.BlockSpec(weight.shape, lambda i, at: (0, 0)),
            ],
            out_specs=pl.BlockSpec((2 * half, local_count * width), lambda i, at: (0, 0)),
        ),
        compiler_params=pltpu.CompilerParams(vmem_limit_bytes=VMEM_LIMIT),
        cost_estimate=pl.CostEstimate(flops=flops, bytes_accessed=8 << 20, transcendentals=0),
    )(at, near, far, w_gate, w_up, total, weight)


def down(at, value, w_down, depth):
    row_count, width = value.shape
    half = row_count // 2
    cuts = 2 if depth % 256 == 0 else 1
    block = depth // cuts
    return pl.pallas_call(
        down_kernel,
        out_shape=(
            jax.ShapeDtypeStruct((half, depth), jnp.float32),
            jax.ShapeDtypeStruct((half, depth), jnp.bfloat16),
        ),
        grid_spec=pltpu.PrefetchScalarGridSpec(
            num_scalar_prefetch=1,
            grid=(cuts,),
            in_specs=[
                pl.BlockSpec((row_count, width), lambda i, at: (0, 0)),
                pl.BlockSpec((width, block), lambda i, at: (0, at[0] * cuts + i)),
            ],
            out_specs=[pl.BlockSpec((half, block), lambda i, at: (0, i))] * 2,
        ),
        compiler_params=pltpu.CompilerParams(vmem_limit_bytes=VMEM_LIMIT),
        cost_estimate=pl.CostEstimate(
            flops=2 * row_count * width * depth, bytes_accessed=4 << 20, transcendentals=0
        ),
    )(at, value, w_down)


def route_weights(expert_ids, gates, hot_list, expert_count, capacity):
    row_count = expert_ids.shape[0]
    numbers = jnp.arange(expert_count, dtype=jnp.int32)
    match = expert_ids[:, :, None] == numbers[None, None, :]
    weight = jnp.sum(jnp.where(match, gates[:, :, None], 0.0), axis=1)
    member = jnp.any(match, axis=1)
    order = jnp.arange(row_count)
    earlier = (order[:, None] > order[None, :]).astype(jnp.bfloat16)
    slot = dot(earlier, member.astype(jnp.bfloat16))
    hot = jnp.any(numbers[:, None] == hot_list[None, :], axis=1)
    kept = jnp.logical_and(member, jnp.logical_or(hot[None, :], slot < capacity))
    return jnp.where(kept, weight, 0.0)


def body(tokens, expert_ids, gates, hot_list, w_gate, w_up, w_down):
    owner_count, seq_count = lax.axis_size("expert"), lax.axis_size("seq")
    chip_count = owner_count // 2
    local_count, feature_count, width = w_gate.shape
    expert_count = local_count * owner_count
    row_count, pick_count = expert_ids.shape
    depth = tokens.shape[1]
    capacity = 3 * row_count * pick_count // (4 * expert_count)
    me, seq = lax.axis_index("expert"), lax.axis_index("seq")

    def over_seq(value, shift):
        if shift == 0:
            return value
        return lax.ppermute(value, "seq", [(i, (i + shift) % seq_count) for i in range(seq_count)])

    def over_chips(value, shift):
        if shift % chip_count == 0:
            return value
        return lax.ppermute(
            value,
            "expert",
            [
                (2 * i + c, 2 * ((i + shift) % chip_count) + c)
                for i in range(chip_count)
                for c in range(2)
            ],
        )

    def over_core(value):
        return lax.ppermute(value, "expert", [(i, i ^ 1) for i in range(owner_count)])

    def gathered(value):
        near = jnp.concatenate([over_chips(value, shift) for shift in range(chip_count)], axis=0)
        return near, over_core(near)

    shifts = [s for k in range(seq_count) for s in {k, (-k) % seq_count} if k <= seq_count // 2]
    weights = route_weights(expert_ids, gates, hot_list, expert_count, capacity)
    pieces = [(shift, over_seq(tokens, shift)) for shift in shifts]
    near_weights, far_weights = gathered(weights.T[None])
    own_weights = lax.dynamic_slice_in_dim(
        jnp.concatenate([near_weights, far_weights], axis=0), me * local_count, local_count, axis=1
    )
    own_weights = jnp.transpose(own_weights, (0, 2, 1)).reshape(-1, local_count)

    total = None
    for number, (shift, piece) in enumerate(pieces):
        near, far = gathered(piece)
        at = ((seq - shift) % seq_count).astype(jnp.int32).reshape(1)
        if number < len(pieces) - 1:
            total = gate_up(at, near, far, w_gate, w_up, total)
        else:
            value = hidden(at, near, far, w_gate, w_up, total, own_weights)

    flat_down = w_down.reshape(local_count * width, feature_count)
    moved = None
    for shift in shifts[::-1]:
        at = ((seq + shift) % seq_count).astype(jnp.int32).reshape(1)
        keep, send = down(at, value, flat_down, depth)
        pair = (keep + over_core(send).astype(jnp.float32)).reshape(chip_count, row_count, depth)
        row = pair[0]
        for chip in range(1, chip_count):
            row = row + over_chips(pair[chip].astype(jnp.bfloat16), -chip).astype(jnp.float32)
        term = row if shift == 0 else over_seq(row.astype(jnp.bfloat16), shift).astype(jnp.float32)
        moved = term if moved is None else moved + term
    return moved.astype(jnp.bfloat16)


def solution(mesh):
    placed = (
        P(("parts", "expert"), "seq"),
        P(("parts", "expert"), None),
        P(("parts", "expert"), None),
        P("parts"),
        P("expert", None, "seq"),
        P("expert", None, "seq"),
        P("expert", "seq", None),
    )
    return jax.shard_map(
        body, mesh=mesh, in_specs=placed, out_specs=P(("parts", "expert"), "seq"), check_vma=False
    )
```

time: 683 us -> 133 us (0.19)
  waiting for transfers between devices: 491 us -> 59.2 us
  local copies, waits for them, and re-layouts: 67.3 us -> 6.65 us
  matrix products: 50.1 us -> 0.11 us
  Pallas kernels: 0 us -> 42.3 us
  other arithmetic: 36.9 us -> 3.76 us
  between operations: 20.4 us -> 0.3 us
  starting transfers between devices: 11.1 us -> 20.6 us
    all_to_all x2 -> x0, waiting for transfers between devices: 206 us -> none  [the longest x1 128 us: body(): lax.all_to_all(partial_value, 'expert', split_axis=0, concat_axis=0, tile...]
    psum x1 -> x0, waiting for transfers between devices: 204 us -> none  [broadcast(): return lax.psum(kept, axis)]
    ppermute x0 -> x24, waiting for transfers between devices: none -> 59.2 us  [the longest x9 31.8 us: over_chips(): lax.ppermute(value, 'expert', [(2 * i + c, 2 * ((i + shift) % chip_count)...]
    gather x7 -> x0, local copies, waits for them, and re-layouts: 58 us -> none  [the longest x6 42.4 us: body(): picked = returned[route_place[:, route_index]].astype(jnp.float32)]
    reduce_scatter x1 -> x0, waiting for transfers between devices: 52.5 us -> none  [body(): moved = lax.psum_scatter(combined, 'seq', scatter_dimension=1, tiled=True)]
    dot_general x8 -> x1, matrix products: 50.1 us -> 0.11 us  [dot(): return jnp.dot(a, b, preferred_element_type=jnp.float32)]
    pallas_call x0 -> x8, Pallas kernels: none -> 42.3 us  [the longest x3 20 us: gate_up(): pl.pallas_call(functools.partial(gate_up_kernel, first), out_shape=jax.Sh...]
    all_gather x1 -> x0, waiting for transfers between devices: 28.1 us -> none  [body(): whole = lax.all_gather(tokens, 'seq', axis=1, tiled=True)]
  transfers between devices with their start and end apart: 5 -> 24, of which waited for: 5 -> 10; matrix products, arithmetic and copies ran while one was open for 16% -> 6% of each run, Pallas kernels for 0% -> 24%
where the time goes in v1:
time: 133 us
  waiting for transfers between devices  59.2 us (45%)
  Pallas kernels  42.3 us (32%)
  starting transfers between devices  20.6 us (15%)
  local copies, waits for them, and re-layouts  6.65 us (5%)
  other arithmetic  3.76 us (3%)
    ppermute x9, waiting for transfers between devices, over_chips(): lax.ppermute(value, 'expert', [(2 * i + c, 2 * ((i + shift) % chip_count)...  31.8 us
    ppermute x6, waiting for transfers between devices, over_seq(): lax.ppermute(value, 'seq', [(i, (i + shift) % seq_count) for i in range(s...  27.3 us
    pallas_call x3, Pallas kernels, gate_up(): pl.pallas_call(functools.partial(gate_up_kernel, first), out_shape=jax.Sh...  20 us
    pallas_call x4, Pallas kernels, down(): pl.pallas_call(down_kernel, out_shape=(jax.ShapeDtypeStruct((half, depth)...  15.6 us
    ppermute x6, starting transfers between devices, over_seq(): lax.ppermute(value, 'seq', [(i, (i + shift) % seq_count) for i in range(s...  9.32 us
    ppermute x9, starting transfers between devices, over_chips(): lax.ppermute(value, 'expert', [(2 * i + c, 2 * ((i + shift) % chip_count)...  8.87 us
    pallas_call x1, Pallas kernels, hidden(): pl.pallas_call(hidden_kernel, out_shape=jax.ShapeDtypeStruct((2 * half, l...  6.74 us
    unnamed x22, local copies, waits for them, and re-layouts  5.55 us
  transfers between devices with their start and end apart: 24, of which 10 were waited for; matrix products, arithmetic and copies ran while one was open for 6% of the time, Pallas kernels for 24%

profile of v1, /device:TPU:0, one launch (start us, length us, event | category | flops | bytes accessed | tf_op | source)
XLA Modules:
  0.0 132.9 jit_solution(10395688064935171176)
XLA Ops:
  0.0 2.9 %collective-permute-start.9 = (bf16[128,1280]{1,0:T(8,128)(2,1)}, bf16[128,1280]{1,0:T(8,128)(2,1)S(1)}, u32[]{:S(2)}, u32[]{:S(2)}) collective-permute-start(bf16[128,1280]{1,0:T(8,128)(2,1)} %param.7), channel_id=1, source_target_pairs={{0,8},{4,12},{8,0},{12,4},{1,9},{5,13},{9,1},{13,5},{2,10},{6,14},... | collective-permute-start | bytes 983048 | tf_op jit(solution)/shard_map/ppermute | solution.py:161
  2.9 1.6 %collective-permute-start.6 = (bf16[128,1280]{1,0:T(8,128)(2,1)}, bf16[128,1280]{1,0:T(8,128)(2,1)}, u32[]{:S(2)}, u32[]{:S(2)}) collective-permute-start(bf16[128,1280]{1,0:T(8,128)(2,1)} %param.7), channel_id=1, source_target_pairs={{0,1},{1,2},{2,3},{3,0},{4,5},{5,6},{6,7},{7,4},{8,9},{9,10},{10,1... | collective-permute-start | bytes 983048 | tf_op jit(solution)/shard_map/ppermute | solution.py:156
  4.5 2.2 %collective-permute-start.3 = (bf16[128,1280]{1,0:T(8,128)(2,1)}, bf16[128,1280]{1,0:T(8,128)(2,1)}, u32[]{:S(2)}, u32[]{:S(2)}) collective-permute-start(bf16[128,1280]{1,0:T(8,128)(2,1)} %param.7), channel_id=1, source_target_pairs={{0,3},{1,0},{2,1},{3,2},{4,7},{5,4},{6,5},{7,6},{8,11},{9,8},{10,9... | collective-permute-start | bytes 983048 | tf_op jit(solution)/shard_map/ppermute | solution.py:156
  11.5 2.0 %collective-permute-done.11 = f32[1,8,128]{2,1,0:T(8,128)S(1)} collective-permute-done((f32[1,8,128]{2,1,0:T(8,128)S(1)}, f32[1,8,128]{2,1,0:T(8,128)S(1)}, u32[]{:S(2)}, u32[]{:S(2)}) %collective-permute-start.11) | collective-permute-done | bytes 4128 | tf_op jit(solution)/shard_map/ppermute | solution.py:161
  14.1 1.6 %collective-permute-done.6 = bf16[128,1280]{1,0:T(8,128)(2,1)} collective-permute-done((bf16[128,1280]{1,0:T(8,128)(2,1)}, bf16[128,1280]{1,0:T(8,128)(2,1)}, u32[]{:S(2)}, u32[]{:S(2)}) %collective-permute-start.6) | collective-permute-done | bytes 327712 | tf_op jit(solution)/shard_map/ppermute | solution.py:156
  17.1 3.6 %collective-permute-done.3 = bf16[128,1280]{1,0:T(8,128)(2,1)} collective-permute-done((bf16[128,1280]{1,0:T(8,128)(2,1)}, bf16[128,1280]{1,0:T(8,128)(2,1)}, u32[]{:S(2)}, u32[]{:S(2)}) %collective-permute-start.3) | collective-permute-done | bytes 327712 | tf_op jit(solution)/shard_map/ppermute | solution.py:156
  22.3 13.0 %collective-permute-done = bf16[128,1280]{1,0:T(8,128)(2,1)} collective-permute-done((bf16[128,1280]{1,0:T(8,128)(2,1)}, bf16[128,1280]{1,0:T(8,128)(2,1)}, u32[]{:S(2)}, u32[]{:S(2)}) %collective-permute-start) | collective-permute-done | bytes 327712 | tf_op jit(solution)/shard_map/ppermute | solution.py:156
  37.7 8.6 %collective-permute-done.1 = bf16[128,1280]{1,0:T(8,128)(2,1)S(1)} collective-permute-done((bf16[128,1280]{1,0:T(8,128)(2,1)}, bf16[128,1280]{1,0:T(8,128)(2,1)S(1)}, u32[]{:S(2)}, u32[]{:S(2)}) %collective-permute-start.1) | collective-permute-done | bytes 327712 | tf_op jit(solution)/shard_map/ppermute | solution.py:161
  48.2 6.1 %shard_map.73.refs_4_ = f32[2,2,512,384]{3,2,1,0:T(8,128)} custom-call(s32[1]{0:T(128)} %bitcast.4.at_ref, bf16[256,1280]{1,0:T(8,128)(2,1)} %copy-done, bf16[256,1280]{1,0:T(8,128)(2,1)} %copy-done.8, bf16[2,5120,384]{2,1,0:T(8,128)(2,1)} %gate_ref.1, bf16[2,5120,384]{2,1,0:T(8,128)(2,1)} %up_ref.1), custom_call_target="tpu_custom_call" | custom-call | flops 2013265920 | bytes 8388608 | tf_op jit(solution)/shard_map/pallas_call | solution.py:60
  54.3 6.9 %shard_map.74.refs_4_ = f32[2,2,512,384]{3,2,1,0:T(8,128)} custom-call(s32[1]{0:T(128)} %bitcast.3.at_ref, bf16[256,1280]{1,0:T(8,128)(2,1)} %copy-done.3, bf16[256,1280]{1,0:T(8,128)(2,1)} %collective-permute-done.8.refs_1_, bf16[2,5120,384]{2,1,0:T(8,128)(2,1)} %gate_ref.1, bf16[2,5120,384]{2,1,0:T(8,128)(2,1)} %up_ref.1, f32[2,2,512,384]{3,2,1,0:T(8,128)} %shard_map.73.refs_4_), custom_call_target="tpu_custom_call" | custom-call | flops 2013265920 | bytes 8388608 | tf_op jit(solution)/shard_map/pallas_call | solution.py:60
  61.2 6.9 %shard_map.75.total_ref = f32[2,2,512,384]{3,2,1,0:T(8,128)} custom-call(s32[1]{0:T(128)} %bitcast.2.at_ref, bf16[256,1280]{1,0:T(8,128)(2,1)} %copy-done.2, bf16[256,1280]{1,0:T(8,128)(2,1)} %collective-permute-done.5.refs_1_, bf16[2,5120,384]{2,1,0:T(8,128)(2,1)} %gate_ref.1, bf16[2,5120,384]{2,1,0:T(8,128)(2,1)} %up_ref.1, ...), custom_call_target="tpu_custom_call" | custom-call | flops 2013265920 | bytes 8388608 | tf_op jit(solution)/shard_map/pallas_call | solution.py:60
  68.2 6.7 %shard_map.76.hidden_ref = bf16[512,768]{1,0:T(8,128)(2,1)} custom-call(s32[1]{0:T(128)} %bitcast.1.at_ref, bf16[256,1280]{1,0:T(8,128)(2,1)} %copy-done.1, bf16[256,1280]{1,0:T(8,128)(2,1)} %collective-permute-done.2.far_ref, bf16[2,5120,384]{2,1,0:T(8,128)(2,1)} %gate_ref.1, bf16[2,5120,384]{2,1,0:T(8,128)(2,1)} %up_ref.1, ...), custom_call_target="tpu_custom_call" | custom-call | flops 2013265920 | bytes 8388608 | tf_op jit(solution)/shard_map/pallas_call | solution.py:81
  74.9 3.9 %shard_map.77 = (f32[256,1280]{1,0:T(8,128)}, bf16[256,1280]{1,0:T(8,128)(2,1)}) custom-call(s32[1]{0:T(128)} %bitcast.at_ref, bf16[512,768]{1,0:T(8,128)(2,1)} %shard_map.76.hidden_ref, bf16[768,5120]{1,0:T(8,128)(2,1)} %bitcast.18), custom_call_target="tpu_custom_call" | custom-call | flops 1006632960 | bytes 4194304 | tf_op jit(solution)/shard_map/pallas_call | solution.py:107
  79.3 3.9 %shard_map.78 = (f32[256,1280]{1,0:T(8,128)}, bf16[256,1280]{1,0:T(8,128)(2,1)}) custom-call(s32[1]{0:T(128)} %bitcast.11.at_ref, bf16[512,768]{1,0:T(8,128)(2,1)} %shard_map.76.hidden_ref, bf16[768,5120]{1,0:T(8,128)(2,1)} %bitcast.19), custom_call_target="tpu_custom_call" | custom-call | flops 1006632960 | bytes 4194304 | tf_op jit(solution)/shard_map/pallas_call | solution.py:107
  83.2 3.9 %shard_map.79 = (f32[256,1280]{1,0:T(8,128)}, bf16[256,1280]{1,0:T(8,128)(2,1)}) custom-call(s32[1]{0:T(128)} %bitcast.12.at_ref, bf16[512,768]{1,0:T(8,128)(2,1)} %shard_map.76.hidden_ref, bf16[768,5120]{1,0:T(8,128)(2,1)} %bitcast.20), custom_call_target="tpu_custom_call" | custom-call | flops 1006632960 | bytes 4194304 | tf_op jit(solution)/shard_map/pallas_call | solution.py:107
  87.6 4.0 %shard_map.80 = (f32[256,1280]{1,0:T(8,128)}, bf16[256,1280]{1,0:T(8,128)(2,1)}) custom-call(s32[1]{0:T(128)} %bitcast.4.at_ref, bf16[512,768]{1,0:T(8,128)(2,1)} %shard_map.76.hidden_ref, bf16[768,5120]{1,0:T(8,128)(2,1)} %bitcast.21), custom_call_target="tpu_custom_call" | custom-call | flops 1006632960 | bytes 4194304 | tf_op jit(solution)/shard_map/pallas_call | solution.py:107
  94.5 1.1 collective-permute-start.20
  96.8 5.6 %collective-permute-done.14 = bf16[128,1280]{1,0:T(8,128)(2,1)S(1)} collective-permute-done((bf16[128,1280]{1,0:T(8,128)(2,1)S(1)}, bf16[128,1280]{1,0:T(8,128)(2,1)S(1)}, u32[]{:S(2)}, u32[]{:S(2)}) %collective-permute-start.14) | collective-permute-done | bytes 327712 | tf_op jit(solution)/shard_map/ppermute | solution.py:161
  102.5 3.2 %collective-permute-start.15 = (bf16[128,1280]{1,0:T(8,128)(2,1)S(1)}, bf16[128,1280]{1,0:T(8,128)(2,1)S(1)}, u32[]{:S(2)}, u32[]{:S(2)}) collective-permute-start(bf16[128,1280]{1,0:T(8,128)(2,1)S(1)} %fusion.8), channel_id=1, source_target_pairs={{0,2},{1,3},{2,0},{3,1},{4,6},{5,7},{6,4},{7,5},{8,10},{9,11},{10,... | collective-permute-start | bytes 983048 | tf_op jit(solution)/shard_map/ppermute | solution.py:156
  105.7 3.8 %collective-permute-done.17 = bf16[128,1280]{1,0:T(8,128)(2,1)S(1)} collective-permute-done((bf16[128,1280]{1,0:T(8,128)(2,1)S(1)}, bf16[128,1280]{1,0:T(8,128)(2,1)S(1)}, u32[]{:S(2)}, u32[]{:S(2)}) %collective-permute-start.17) | collective-permute-done | bytes 327712 | tf_op jit(solution)/shard_map/ppermute | solution.py:161
  109.8 6.7 %collective-permute-done.20 = bf16[128,1280]{1,0:T(8,128)(2,1)S(1)} collective-permute-done((bf16[128,1280]{1,0:T(8,128)(2,1)S(1)}, bf16[128,1280]{1,0:T(8,128)(2,1)S(1)}, u32[]{:S(2)}, u32[]{:S(2)}) %collective-permute-start.20) | collective-permute-done | bytes 327712 | tf_op jit(solution)/shard_map/ppermute | solution.py:161
  116.5 1.3 collective-permute-start.21
  117.8 5.2 %collective-permute-done.23 = bf16[128,1280]{1,0:T(8,128)(2,1)S(1)} collective-permute-done((bf16[128,1280]{1,0:T(8,128)(2,1)S(1)}, bf16[128,1280]{1,0:T(8,128)(2,1)S(1)}, u32[]{:S(2)}, u32[]{:S(2)}) %collective-permute-start.23) | collective-permute-done | bytes 327712 | tf_op jit(solution)/shard_map/ppermute | solution.py:161
  123.0 9.0 %collective-permute-done.18 = bf16[128,1280]{1,0:T(8,128)(2,1)S(1)} collective-permute-done((bf16[128,1280]{1,0:T(8,128)(2,1)S(1)}, bf16[128,1280]{1,0:T(8,128)(2,1)S(1)}, u32[]{:S(2)}, u32[]{:S(2)}) %collective-permute-start.18) | collective-permute-done | bytes 327712 | tf_op jit(solution)/shard_map/ppermute | solution.py:156
  (77 shorter events, 18.9 us)
Async XLA Ops:
  0.0 13.5 %collective-permute-start.9 = (bf16[128,1280]{1,0:T(8,128)(2,1)}, bf16[128,1280]{1,0:T(8,128)(2,1)S(1)}, u32[]{:S(2)}, u32[]{:S(2)}) collective-permute-start(bf16[128,1280]{1,0:T(8,128)(2,1)} %param.7), channel_id=1, source_target_pairs={{0,8},{4,12},{8,0},{12,4},{1,9},{5,13},{9,1},{13,5},{2,10},{6,14},... | collective-permute-start | bytes 983048 | tf_op jit(solution)/shard_map/ppermute | solution.py:161
  2.9 12.8 %collective-permute-start.6 = (bf16[128,1280]{1,0:T(8,128)(2,1)}, bf16[128,1280]{1,0:T(8,128)(2,1)}, u32[]{:S(2)}, u32[]{:S(2)}) collective-permute-start(bf16[128,1280]{1,0:T(8,128)(2,1)} %param.7), channel_id=1, source_target_pairs={{0,1},{1,2},{2,3},{3,0},{4,5},{5,6},{6,7},{7,4},{8,9},{9,10},{10,1... | collective-permute-start | bytes 983048 | tf_op jit(solution)/shard_map/ppermute | solution.py:156
  4.5 16.2 %collective-permute-start.3 = (bf16[128,1280]{1,0:T(8,128)(2,1)}, bf16[128,1280]{1,0:T(8,128)(2,1)}, u32[]{:S(2)}, u32[]{:S(2)}) collective-permute-start(bf16[128,1280]{1,0:T(8,128)(2,1)} %param.7), channel_id=1, source_target_pairs={{0,3},{1,0},{2,1},{3,2},{4,7},{5,4},{6,5},{7,6},{8,11},{9,8},{10,9... | collective-permute-start | bytes 983048 | tf_op jit(solution)/shard_map/ppermute | solution.py:156
  6.8 28.6 %collective-permute-start = (bf16[128,1280]{1,0:T(8,128)(2,1)}, bf16[128,1280]{1,0:T(8,128)(2,1)}, u32[]{:S(2)}, u32[]{:S(2)}) collective-permute-start(bf16[128,1280]{1,0:T(8,128)(2,1)} %param.7), channel_id=1, source_target_pairs={{0,2},{1,3},{2,0},{3,1},{4,6},{5,7},{6,4},{7,5},{8,10},{9,11},{10,... | collective-permute-start | bytes 983048 | tf_op jit(solution)/shard_map/ppermute | solution.py:156
  9.8 3.7 %collective-permute-start.11 = (f32[1,8,128]{2,1,0:T(8,128)S(1)}, f32[1,8,128]{2,1,0:T(8,128)S(1)}, u32[]{:S(2)}, u32[]{:S(2)}) collective-permute-start(f32[1,8,128]{2,1,0:T(8,128)S(1)} %fusion.3), channel_id=1, source_target_pairs={{0,8},{4,12},{8,0},{12,4},{1,9},{5,13},{9,1},{13,5},{2,10},{6,14},... | collective-permute-start | bytes 12296 | tf_op jit(solution)/shard_map/ppermute | solution.py:161
  13.5 32.9 %collective-permute-start.12 = (f32[2,8,128]{2,1,0:T(8,128)S(1)}, f32[2,8,128]{2,1,0:T(8,128)S(1)}, u32[]{:S(2)}, u32[]{:S(2)}) collective-permute-start(f32[2,8,128]{2,1,0:T(8,128)S(1)} %pad_maximum_fusion), channel_id=1, source_target_pairs={{0,4},{4,0},{8,12},{12,8},{1,5},{5,1},{9,13},{13,9},{2,6},{6,2},{1... | collective-permute-start | bytes 24584 | tf_op jit(solution)/shard_map/ppermute | solution.py:172
  13.5 33.8 %collective-permute-start.10 = (bf16[256,1280]{1,0:T(8,128)(2,1)S(1)}, bf16[256,1280]{1,0:T(8,128)(2,1)S(1)}, u32[]{:S(2)}, u32[]{:S(2)}) collective-permute-start(bf16[256,1280]{1,0:T(8,128)(2,1)S(1)} %constant_dynamic-update-slice_fusion.6.refs_0_), channel_id=1, source_target_pairs={{0,4},{4,0},{8,12},{12,8},{1,5},{5,1},{9,13},{13,9},{2,6},{6,2},{1... | collective-permute-start | bytes 1966088 | tf_op jit(solution)/shard_map/ppermute | solution.py:172
  16.7 20.3 %collective-permute-start.7 = (bf16[128,1280]{1,0:T(8,128)(2,1)}, bf16[128,1280]{1,0:T(8,128)(2,1)S(1)}, u32[]{:S(2)}, u32[]{:S(2)}) collective-permute-start(bf16[128,1280]{1,0:T(8,128)(2,1)} %collective-permute-done.6), channel_id=1, source_target_pairs={{0,8},{4,12},{8,0},{12,4},{1,9},{5,13},{9,1},{13,5},{2,10},{6,14},... | collective-permute-start | bytes 983048 | tf_op jit(solution)/shard_map/ppermute | solution.py:161
  21.7 15.4 %collective-permute-start.4 = (bf16[128,1280]{1,0:T(8,128)(2,1)}, bf16[128,1280]{1,0:T(8,128)(2,1)S(1)}, u32[]{:S(2)}, u32[]{:S(2)}) collective-permute-start(bf16[128,1280]{1,0:T(8,128)(2,1)} %collective-permute-done.3), channel_id=1, source_target_pairs={{0,8},{4,12},{8,0},{12,4},{1,9},{5,13},{9,1},{13,5},{2,10},{6,14},... | collective-permute-start | bytes 983048 | tf_op jit(solution)/shard_map/ppermute | solution.py:161
  36.4 9.9 %collective-permute-start.1 = (bf16[128,1280]{1,0:T(8,128)(2,1)}, bf16[128,1280]{1,0:T(8,128)(2,1)S(1)}, u32[]{:S(2)}, u32[]{:S(2)}) collective-permute-start(bf16[128,1280]{1,0:T(8,128)(2,1)} %collective-permute-done), channel_id=1, source_target_pairs={{0,8},{4,12},{8,0},{12,4},{1,9},{5,13},{9,1},{13,5},{2,10},{6,14},... | collective-permute-start | bytes 983048 | tf_op jit(solution)/shard_map/ppermute | solution.py:161
  37.0 17.3 %collective-permute-start.8 = (bf16[256,1280]{1,0:T(8,128)(2,1)S(1)}, bf16[256,1280]{1,0:T(8,128)(2,1)}, u32[]{:S(2)}, u32[]{:S(2)}) collective-permute-start(bf16[256,1280]{1,0:T(8,128)(2,1)S(1)} %constant_dynamic-update-slice_fusion.4.refs_0_), channel_id=1, source_target_pairs={{0,4},{4,0},{8,12},{12,8},{1,5},{5,1},{9,13},{13,9},{2,6},{6,2},{1... | collective-permute-start | bytes 1966088 | tf_op jit(solution)/shard_map/ppermute | solution.py:172
  37.2 24.1 %collective-permute-start.5 = (bf16[256,1280]{1,0:T(8,128)(2,1)S(1)}, bf16[256,1280]{1,0:T(8,128)(2,1)}, u32[]{:S(2)}, u32[]{:S(2)}) collective-permute-start(bf16[256,1280]{1,0:T(8,128)(2,1)S(1)} %constant_dynamic-update-slice_fusion.2.refs_0_), channel_id=1, source_target_pairs={{0,4},{4,0},{8,12},{12,8},{1,5},{5,1},{9,13},{13,9},{2,6},{6,2},{1... | collective-permute-start | bytes 1966088 | tf_op jit(solution)/shard_map/ppermute | solution.py:172
  46.3 21.8 %collective-permute-start.2 = (bf16[256,1280]{1,0:T(8,128)(2,1)S(1)}, bf16[256,1280]{1,0:T(8,128)(2,1)}, u32[]{:S(2)}, u32[]{:S(2)}) collective-permute-start(bf16[256,1280]{1,0:T(8,128)(2,1)S(1)} %constant_dynamic-update-slice_fusion.near_ref), channel_id=1, source_target_pairs={{0,4},{4,0},{8,12},{12,8},{1,5},{5,1},{9,13},{13,9},{2,6},{6,2},{1... | collective-permute-start | bytes 1966088 | tf_op jit(solution)/shard_map/ppermute | solution.py:172
  78.8 12.8 %collective-permute-start.13 = (bf16[256,1280]{1,0:T(8,128)(2,1)}, bf16[256,1280]{1,0:T(8,128)(2,1)S(1)}, u32[]{:S(2)}, u32[]{:S(2)}) collective-permute-start(bf16[256,1280]{1,0:T(8,128)(2,1)} %get-tuple-element.14), channel_id=1, source_target_pairs={{0,4},{4,0},{8,12},{12,8},{1,5},{5,1},{9,13},{13,9},{2,6},{6,2},{1... | collective-permute-start | bytes 1966088 | tf_op jit(solution)/shard_map/ppermute | solution.py:172
  83.2 9.3 %collective-permute-start.16 = (bf16[256,1280]{1,0:T(8,128)(2,1)}, bf16[256,1280]{1,0:T(8,128)(2,1)S(1)}, u32[]{:S(2)}, u32[]{:S(2)}) collective-permute-start(bf16[256,1280]{1,0:T(8,128)(2,1)} %get-tuple-element.16), channel_id=1, source_target_pairs={{0,4},{4,0},{8,12},{12,8},{1,5},{5,1},{9,13},{13,9},{2,6},{6,2},{1... | collective-permute-start | bytes 1966088 | tf_op jit(solution)/shard_map/ppermute | solution.py:172
  87.1 7.1 %collective-permute-start.19 = (bf16[256,1280]{1,0:T(8,128)(2,1)}, bf16[256,1280]{1,0:T(8,128)(2,1)S(1)}, u32[]{:S(2)}, u32[]{:S(2)}) collective-permute-start(bf16[256,1280]{1,0:T(8,128)(2,1)} %get-tuple-element.18), channel_id=1, source_target_pairs={{0,4},{4,0},{8,12},{12,8},{1,5},{5,1},{9,13},{13,9},{2,6},{6,2},{1... | collective-permute-start | bytes 1966088 | tf_op jit(solution)/shard_map/ppermute | solution.py:172
  91.5 4.0 %collective-permute-start.22 = (bf16[256,1280]{1,0:T(8,128)(2,1)}, bf16[256,1280]{1,0:T(8,128)(2,1)S(1)}, u32[]{:S(2)}, u32[]{:S(2)}) collective-permute-start(bf16[256,1280]{1,0:T(8,128)(2,1)} %get-tuple-element.20), channel_id=1, source_target_pairs={{0,4},{4,0},{8,12},{12,8},{1,5},{5,1},{9,13},{13,9},{2,6},{6,2},{1... | collective-permute-start | bytes 1966088 | tf_op jit(solution)/shard_map/ppermute | solution.py:172
  91.8 10.6 %collective-permute-start.14 = (bf16[128,1280]{1,0:T(8,128)(2,1)S(1)}, bf16[128,1280]{1,0:T(8,128)(2,1)S(1)}, u32[]{:S(2)}, u32[]{:S(2)}) collective-permute-start(bf16[128,1280]{1,0:T(8,128)(2,1)S(1)} %slice.73), channel_id=1, source_target_pairs={{0,8},{4,12},{8,0},{12,4},{1,9},{5,13},{9,1},{13,5},{2,10},{6,14},... | collective-permute-start | bytes 983048 | tf_op jit(solution)/shard_map/ppermute | solution.py:161
  93.2 16.3 %collective-permute-start.17 = (bf16[128,1280]{1,0:T(8,128)(2,1)S(1)}, bf16[128,1280]{1,0:T(8,128)(2,1)S(1)}, u32[]{:S(2)}, u32[]{:S(2)}) collective-permute-start(bf16[128,1280]{1,0:T(8,128)(2,1)S(1)} %slice.72), channel_id=1, source_target_pairs={{0,8},{4,12},{8,0},{12,4},{1,9},{5,13},{9,1},{13,5},{2,10},{6,14},... | collective-permute-start | bytes 983048 | tf_op jit(solution)/shard_map/ppermute | solution.py:161
  94.5 22.0 %collective-permute-start.20 = (bf16[128,1280]{1,0:T(8,128)(2,1)S(1)}, bf16[128,1280]{1,0:T(8,128)(2,1)S(1)}, u32[]{:S(2)}, u32[]{:S(2)}) collective-permute-start(bf16[128,1280]{1,0:T(8,128)(2,1)S(1)} %slice.71), channel_id=1, source_target_pairs={{0,8},{4,12},{8,0},{12,4},{1,9},{5,13},{9,1},{13,5},{2,10},{6,14},... | collective-permute-start | bytes 983048 | tf_op jit(solution)/shard_map/ppermute | solution.py:161
  95.8 27.2 %collective-permute-start.23 = (bf16[128,1280]{1,0:T(8,128)(2,1)S(1)}, bf16[128,1280]{1,0:T(8,128)(2,1)S(1)}, u32[]{:S(2)}, u32[]{:S(2)}) collective-permute-start(bf16[128,1280]{1,0:T(8,128)(2,1)S(1)} %slice.70), channel_id=1, source_target_pairs={{0,8},{4,12},{8,0},{12,4},{1,9},{5,13},{9,1},{13,5},{2,10},{6,14},... | collective-permute-start | bytes 983048 | tf_op jit(solution)/shard_map/ppermute | solution.py:161
  102.5 20.5 %collective-permute-start.15 = (bf16[128,1280]{1,0:T(8,128)(2,1)S(1)}, bf16[128,1280]{1,0:T(8,128)(2,1)S(1)}, u32[]{:S(2)}, u32[]{:S(2)}) collective-permute-start(bf16[128,1280]{1,0:T(8,128)(2,1)S(1)} %fusion.8), channel_id=1, source_target_pairs={{0,2},{1,3},{2,0},{3,1},{4,6},{5,7},{6,4},{7,5},{8,10},{9,11},{10,... | collective-permute-start | bytes 983048 | tf_op jit(solution)/shard_map/ppermute | solution.py:156
  109.5 22.5 %collective-permute-start.18 = (bf16[128,1280]{1,0:T(8,128)(2,1)S(1)}, bf16[128,1280]{1,0:T(8,128)(2,1)S(1)}, u32[]{:S(2)}, u32[]{:S(2)}) collective-permute-start(bf16[128,1280]{1,0:T(8,128)(2,1)S(1)} %fusion.7), channel_id=1, source_target_pairs={{0,3},{1,0},{2,1},{3,2},{4,7},{5,4},{6,5},{7,6},{8,11},{9,8},{10,9... | collective-permute-start | bytes 983048 | tf_op jit(solution)/shard_map/ppermute | solution.py:156
  116.5 15.4 %collective-permute-start.21 = (bf16[128,1280]{1,0:T(8,128)(2,1)S(1)}, bf16[128,1280]{1,0:T(8,128)(2,1)S(1)}, u32[]{:S(2)}, u32[]{:S(2)}) collective-permute-start(bf16[128,1280]{1,0:T(8,128)(2,1)S(1)} %fusion.6), channel_id=1, source_target_pairs={{0,1},{1,2},{2,3},{3,0},{4,5},{5,6},{6,7},{7,4},{8,9},{9,10},{10,1... | collective-permute-start | bytes 983048 | tf_op jit(solution)/shard_map/ppermute | solution.py:156
  (9 other events, 75.2 us)

commit v2 on v1

v2 whole, which is shorter than its diff:
```python
import functools

import jax
import jax.numpy as jnp
from jax import lax
from jax.experimental import pallas as pl
from jax.experimental.pallas import tpu as pltpu
from jax.sharding import PartitionSpec as P

VMEM_LIMIT = 16 * 1024 * 1024
COST = 8000000000
VMEM = pl.BlockSpec(memory_space=pltpu.VMEM)
HBM = pl.BlockSpec(memory_space=pltpu.HBM)
SMEM = pl.BlockSpec(memory_space=pltpu.SMEM)


def dot(a, b):
    return jnp.dot(a, b, preferred_element_type=jnp.float32)


def call(kernel, out_shape, in_specs, cost=COST, **more):
    many = isinstance(out_shape, (tuple, list))
    return pl.pallas_call(
        kernel,
        out_shape=out_shape,
        in_specs=in_specs,
        out_specs=[VMEM] * len(out_shape) if many else VMEM,
        compiler_params=pltpu.CompilerParams(vmem_limit_bytes=VMEM_LIMIT),
        cost_estimate=pl.CostEstimate(flops=cost, bytes_accessed=cost, transcendentals=0),
        **more,
    )


def in_hbm(value):
    return pltpu.with_memory_space_constraint(value, pltpu.HBM)


def in_vmem(value):
    return pltpu.with_memory_space_constraint(value, pltpu.VMEM)


def load_parts(sources, part_refs, sems, block):
    local_count, _, width = sources[0].shape
    depth = part_refs[0].shape[1]
    rows = pl.ds(pl.multiple_of(block * depth, depth), depth)
    loads = []
    for index in range(local_count):
        copies = []
        for side, source in enumerate(sources):
            if len(part_refs) == 1:
                target = part_refs[0].at[index, :, side * width : (side + 1) * width]
            else:
                target = part_refs[side].at[index]
            copies.append(
                pltpu.make_async_copy(source.at[index, rows], target, sems.at[2 * index + side])
            )
        loads.append(copies)
    return loads


def load_down(source, part_ref, sems, block):
    depth = part_ref.shape[2]
    columns = pl.ds(pl.multiple_of(block * depth, depth), depth)
    return [
        pltpu.make_async_copy(source.at[index, :, columns], part_ref.at[index], sems.at[index])
        for index in range(source.shape[0])
    ]


def start(copies):
    for copy in copies:
        copy.start()


def wait(copies):
    for copy in copies:
        copy.wait()


def products(rows, part_refs, index):
    parts = [dot(rows, part_ref[index]) for part_ref in part_refs]
    return parts[0] if len(parts) == 1 else jnp.concatenate(parts, axis=1)


def gate_up_kernel(first, at_ref, near_ref, far_ref, gate_ref, up_ref, *refs):
    total_ref, refs = (None, refs) if first else (refs[0], refs[1:])
    out_ref, part_refs, sems = refs[0], refs[1:-1], refs[-1]
    loads = load_parts([gate_ref, up_ref], part_refs, sems, at_ref[0])
    for copies in loads:
        start(copies)
    rows = jnp.concatenate([near_ref[...], far_ref[...]], axis=0)
    for index, copies in enumerate(loads):
        wait(copies)
        value = products(rows, part_refs, index)
        out_ref[index] = value if first else value + total_ref[index]


def down_product(value, part_ref, keep_ref, send_ref):
    half, width = keep_ref.shape[0], part_ref.shape[1]
    if width % 128 == 0:
        parts = [part_ref[index] for index in range(part_ref.shape[0])]
        result = dot(value, jnp.concatenate(parts, axis=0))
    else:
        result = 0.0
        for index in range(part_ref.shape[0]):
            result += dot(value[:, index * width : (index + 1) * width], part_ref[index])
    send_ref[...] = result[half:].astype(jnp.bfloat16)
    keep_ref[...] = result[:half]


def last_load_kernel(at_ref, gate_ref, up_ref, down_ref, *refs):
    part_refs, (down_part, sems, down_sems) = refs[:-3], refs[-3:]
    loads = load_parts([gate_ref, up_ref], part_refs, sems, at_ref[0])
    loads.append(load_down(down_ref, down_part, down_sems, at_ref[1]))
    for copies in loads:
        start(copies)
    for copies in loads:
        wait(copies)


def hidden_kernel(near_ref, far_ref, total_ref, weight_ref, *refs):
    part_refs, (down_part, out_ref, keep_ref, send_ref) = refs[:-4], refs[-4:]
    width = total_ref.shape[2] // 2
    rows = jnp.concatenate([near_ref[...], far_ref[...]], axis=0)
    for index in range(total_ref.shape[0]):
        value = products(rows, part_refs, index) + total_ref[index]
        gate_value, up_value = value[:, :width], value[:, width:]
        value = gate_value / (1.0 + jnp.exp(-gate_value)) * up_value
        value = value * weight_ref[:, index : index + 1]
        out_ref[:, index * width : (index + 1) * width] = value.astype(jnp.bfloat16)
    down_product(out_ref[...], down_part, keep_ref, send_ref)


def down_kernel(at_ref, hidden_ref, down_ref, keep_ref, send_ref, part_ref, sems):
    copies = load_down(down_ref, part_ref, sems, at_ref[0])
    start(copies)
    wait(copies)
    down_product(hidden_ref[...], part_ref, keep_ref, send_ref)


def part_scratch(w_gate, depth):
    local_count, _, width = w_gate.shape
    aligned = width % 128 == 0
    shape = (local_count, depth, 2 * width if aligned else width)
    return [pltpu.VMEM(shape, w_gate.dtype)] * (1 if aligned else 2)


def down_scratch(w_down, depth):
    return pltpu.VMEM((w_down.shape[0], w_down.shape[1], depth), w_down.dtype)


def down_shapes(half, depth):
    return [
        jax.ShapeDtypeStruct((half, depth), jnp.float32),
        jax.ShapeDtypeStruct((half, depth), jnp.bfloat16),
    ]


def gate_up(at, near, far, w_gate, w_up, total):
    local_count, _, width = w_gate.shape
    half, depth = near.shape
    totals = [] if total is None else [total]
    return call(
        functools.partial(gate_up_kernel, total is None),
        jax.ShapeDtypeStruct((local_count, 2 * half, 2 * width), jnp.float32),
        [SMEM, VMEM, VMEM, HBM, HBM] + [VMEM] * len(totals),
        scratch_shapes=part_scratch(w_gate, depth) + [pltpu.SemaphoreType.DMA((2 * local_count,))],
    )(at, near, far, in_hbm(w_gate), in_hbm(w_up), *totals)


def last_load(at, w_gate, w_up, w_down, depth):
    local_count = w_gate.shape[0]
    return call(
        last_load_kernel,
        part_scratch(w_gate, depth) + [down_scratch(w_down, depth)],
        [SMEM, HBM, HBM, HBM],
        scratch_shapes=[
            pltpu.SemaphoreType.DMA((2 * local_count,)),
            pltpu.SemaphoreType.DMA((local_count,)),
        ],
    )(at, in_hbm(w_gate), in_hbm(w_up), in_hbm(w_down))


def hidden(near, far, total, weight, parts):
    local_count, row_count, width = total.shape
    half, depth = near.shape
    return call(
        hidden_kernel,
        [jax.ShapeDtypeStruct((row_count, local_count * width // 2), jnp.bfloat16)]
        + down_shapes(half, depth),
        [VMEM] * (4 + len(parts)),
    )(near, far, total, weight, *map(in_vmem, parts))


def down(at, value, w_down, depth):
    return call(
        down_kernel,
        down_shapes(value.shape[0] // 2, depth),
        [SMEM, VMEM, HBM],
        scratch_shapes=[
            down_scratch(w_down, depth),
            pltpu.SemaphoreType.DMA((w_down.shape[0],)),
        ],
    )(at, value, in_hbm(w_down))


def route_weights(expert_ids, gates, hot_list, expert_count, capacity):
    row_count = expert_ids.shape[0]
    numbers = jnp.arange(expert_count, dtype=jnp.int32)
    match = expert_ids[:, :, None] == numbers[None, None, :]
    weight = jnp.sum(jnp.where(match, gates[:, :, None], 0.0), axis=1)
    member = jnp.any(match, axis=1)
    order = jnp.arange(row_count)
    earlier = (order[:, None] > order[None, :]).astype(jnp.bfloat16)
    slot = dot(earlier, member.astype(jnp.bfloat16))
    hot = jnp.any(numbers[:, None] == hot_list[None, :], axis=1)
    kept = jnp.logical_and(member, jnp.logical_or(hot[None, :], slot < capacity))
    return jnp.where(kept, weight, 0.0)


def body(tokens, expert_ids, gates, hot_list, w_gate, w_up, w_down):
    owner_count, seq_count = lax.axis_size("expert"), lax.axis_size("seq")
    chip_count = owner_count // 2
    local_count, feature_count, width = w_gate.shape
    expert_count = local_count * owner_count
    row_count, pick_count = expert_ids.shape
    depth = tokens.shape[1]
    capacity = 3 * row_count * pick_count // (4 * expert_count)
    me, seq = lax.axis_index("expert"), lax.axis_index("seq")

    def over_seq(value, flip):
        return lax.ppermute(value, "seq", [(i, i ^ flip) for i in range(seq_count)])

    def over_chips(value, shift):
        if shift % chip_count == 0:
            return value
        return lax.ppermute(
            value,
            "expert",
            [
                (2 * i + c, 2 * ((i + shift) % chip_count) + c)
                for i in range(chip_count)
                for c in range(2)
            ],
        )

    def over_core(value):
        return lax.ppermute(value, "expert", [(i, i ^ 1) for i in range(owner_count)])

    def gathered(value):
        near = jnp.concatenate([over_chips(value, shift) for shift in range(chip_count)], axis=0)
        return near, over_core(near)

    weights = route_weights(expert_ids, gates, hot_list, expert_count, capacity)
    near_weights, far_weights = gathered(weights.T[None])
    own_weights = lax.dynamic_slice_in_dim(
        jnp.concatenate([near_weights, far_weights], axis=0), me * local_count, local_count, axis=1
    )
    own_weights = jnp.transpose(own_weights, (0, 2, 1)).reshape(-1, local_count)

    after = lax.optimization_barrier

    def places(flip):
        return (seq ^ flip).astype(jnp.int32).reshape(1)

    def both_chips(piece):
        return jnp.concatenate([over_chips(piece, c) for c in range(chip_count)], axis=0)

    gates = {'q1': ['p2'], 'm1': ['weights'], 'm2': ['t0'], 'm3': ['t2'], 'a0': ['t2']}
    last = seq_count - 1
    have = {"p0": tokens, "weights": own_weights, "w": weights}

    def both_chips(piece):
        return jnp.concatenate([over_chips(piece, c) for c in range(chip_count)], axis=0)

    def get(name):
        if name in have:
            return have[name]
        kind, flip = name[0], int(name[1:])
        if kind == "p":
            value = over_seq(get("p%d" % (flip & (flip - 1))), flip & -flip)
        elif kind == "q":
            value = get("p%d" % flip)
        elif kind == "n":
            value = both_chips(get("q%d" % flip))
        elif kind == "m":
            value = get("n%d" % flip)
        elif kind == "a":
            value = jnp.concatenate([places(last), places(last)])
        elif kind == "l":
            value = last_load(get("a0"), w_gate, w_up, w_down, depth)
        elif kind == "c":
            value = over_core(get("m%d" % flip))
        else:
            pair = get("m%d" % flip), get("c%d" % flip)
            before = get("t%d" % (flip - 1)) if flip else None
            if flip < last:
                value = gate_up(places(flip), *pair, w_gate, w_up, before)
            else:
                value, *have["first"] = hidden(*pair, before, get("weights"), get("l0"))
        for other in gates.get(name, ()):
            value, have[other] = after((value, get(other)))
        have[name] = value
        return value

    value = get("t%d" % last)
    pairs = {}
    for number, flip in enumerate(range(seq_count)[::-1]):
        if number >= 2:
            value, pairs[flip + 2] = after((value, pairs[flip + 2]))
        keep, send = have["first"] if flip == last else down(places(flip), value, w_down, depth)
        pairs[flip] = keep + over_core(send).astype(jnp.float32)
    rows = {}
    for flip in range(seq_count)[::-1]:
        pair = pairs[flip].reshape(chip_count, row_count, depth)
        row = pair[0]
        for chip in range(1, chip_count):
            row = row + over_chips(pair[chip].astype(jnp.bfloat16), -chip).astype(jnp.float32)
        rows[flip] = row
    for flip in range(1, seq_count)[::-1]:
        moved = over_seq(rows[flip].astype(jnp.bfloat16), flip & -flip).astype(jnp.float32)
        rows[flip & (flip - 1)] = rows[flip & (flip - 1)] + moved
    moved = rows[0]
    return moved.astype(jnp.bfloat16)


def solution(mesh):
    placed = (
        P(("parts", "expert"), "seq"),
        P(("parts", "expert"), None),
        P(("parts", "expert"), None),
        P("parts"),
        P("expert", None, "seq"),
        P("expert", None, "seq"),
        P("expert", "seq", None),
    )
    return jax.shard_map(
        body, mesh=mesh, in_specs=placed, out_specs=P(("parts", "expert"), "seq"), check_vma=False
    )
```

time: 133 us -> 104 us (0.78)
  waiting for transfers between devices: 59.2 us -> 44.5 us
  Pallas kernels: 42.3 us -> 28.8 us
  local copies, waits for them, and re-layouts: 6.65 us -> 1.31 us
  starting transfers between devices: 20.6 us -> 24.3 us
    pallas_call x8, Pallas kernels: 42.3 us -> 28.8 us  [the longest x3 13.7 us: gate_up(): call(functools.partial(gate_up_kernel, total is None), jax.ShapeDtypeStru...]
    ppermute x6, waiting for transfers between devices: 27.3 us -> 19.4 us  [over_seq(): return lax.ppermute(value, 'seq', [(i, i ^ flip) for i in range(seq_count)])]
    ppermute x9, waiting for transfers between devices: 31.8 us -> 25.2 us  [over_chips(): lax.ppermute(value, 'expert', [(2 * i + c, 2 * ((i + shift) % chip_count)...]
    unnamed x22 -> x1, local copies, waits for them, and re-layouts: 5.55 us -> 0.99 us
    ppermute x6, starting transfers between devices: 9.32 us -> 12.6 us  [over_seq(): return lax.ppermute(value, 'seq', [(i, i ^ flip) for i in range(seq_count)])]
    ppermute x9, starting transfers between devices: 8.87 us -> 10.4 us  [over_chips(): lax.ppermute(value, 'expert', [(2 * i + c, 2 * ((i + shift) % chip_count)...]
  transfers between devices with their start and end apart: 24 -> 24, of which waited for: 10 -> 14; matrix products, arithmetic and copies ran while one was open for 6% -> 4% of each run, Pallas kernels for 24% -> 20%
where the time goes in v2:
time: 104 us; the launch traced here: 103 us
  waiting for transfers between devices  44.5 us (43%)
  Pallas kernels  28.8 us (28%)
  starting transfers between devices  24.3 us (23%)
  other arithmetic  3.95 us (4%)
  local copies, waits for them, and re-layouts  1.31 us (1%)
    ppermute x9, waiting for transfers between devices, over_chips(): lax.ppermute(value, 'expert', [(2 * i + c, 2 * ((i + shift) % chip_count)...  25.2 us
    ppermute x6, waiting for transfers between devices, over_seq(): return lax.ppermute(value, 'seq', [(i, i ^ flip) for i in range(seq_count)])  19.4 us
    pallas_call x3, Pallas kernels, gate_up(): call(functools.partial(gate_up_kernel, total is None), jax.ShapeDtypeStru...  13.7 us
    ppermute x6, starting transfers between devices, over_seq(): return lax.ppermute(value, 'seq', [(i, i ^ flip) for i in range(seq_count)])  12.6 us
    ppermute x9, starting transfers between devices, over_chips(): lax.ppermute(value, 'expert', [(2 * i + c, 2 * ((i + shift) % chip_count)...  10.4 us
    pallas_call x3, Pallas kernels, down(): call(down_kernel, down_shapes(value.shape[0] // 2, depth), [SMEM, VMEM, H...  8.28 us
    pallas_call x1, Pallas kernels, hidden(): call(hidden_kernel, [jax.ShapeDtypeStruct((row_count, local_count * width...  3.54 us
    pallas_call x1, Pallas kernels, last_load(): call(last_load_kernel, part_scratch(w_gate, depth) + [down_scratch(w_down...  3.28 us
  transfers between devices with their start and end apart: 24, of which 14 were waited for; matrix products, arithmetic and copies ran while one was open for 4% of the time, Pallas kernels for 20%

profile of v2, /device:TPU:0, one launch (start us, length us, event | category | flops | bytes accessed | tf_op | source)
XLA Modules:
  0.0 103.2 jit_solution(11696754359918109396)
XLA Ops:
  0.0 2.9 %collective-permute-start.4 = (bf16[128,1280]{1,0:T(8,128)(2,1)}, bf16[128,1280]{1,0:T(8,128)(2,1)S(1)}, u32[]{:S(2)}, u32[]{:S(2)}) collective-permute-start(bf16[128,1280]{1,0:T(8,128)(2,1)} %param.7), channel_id=1, source_target_pairs={{0,8},{4,12},{8,0},{12,4},{1,9},{5,13},{9,1},{13,5},{2,10},{6,14},... | collective-permute-start | bytes 983048 | tf_op jit(solution)/shard_map/ppermute | solution.py:237
  2.9 2.6 %collective-permute-start = (bf16[128,1280]{1,0:T(8,128)(2,1)}, bf16[128,1280]{1,0:T(8,128)(2,1)S(1)}, u32[]{:S(2)}, u32[]{:S(2)}) collective-permute-start(bf16[128,1280]{1,0:T(8,128)(2,1)} %param.7), channel_id=1, source_target_pairs={{0,2},{1,3},{2,0},{3,1},{4,6},{5,7},{6,4},{7,5},{8,10},{9,11},{10,... | collective-permute-start | bytes 983048 | tf_op jit(solution)/shard_map/ppermute | solution.py:232
  5.5 1.6 %collective-permute-start.7 = (bf16[128,1280]{1,0:T(8,128)(2,1)}, bf16[128,1280]{1,0:T(8,128)(2,1)S(1)}, u32[]{:S(2)}, u32[]{:S(2)}) collective-permute-start(bf16[128,1280]{1,0:T(8,128)(2,1)} %param.7), channel_id=1, source_target_pairs={{0,1},{1,0},{2,3},{3,2},{4,5},{5,4},{6,7},{7,6},{8,9},{9,8},{10,11... | collective-permute-start | bytes 983048 | tf_op jit(solution)/shard_map/ppermute | solution.py:232
  11.0 2.1 %collective-permute-done.9 = f32[1,8,128]{2,1,0:T(8,128)S(1)} collective-permute-done((f32[1,8,128]{2,1,0:T(8,128)S(1)}, f32[1,8,128]{2,1,0:T(8,128)S(1)}, u32[]{:S(2)}, u32[]{:S(2)}) %collective-permute-start.9) | collective-permute-done | bytes 4128 | tf_op jit(solution)/shard_map/ppermute | solution.py:237
  13.0 7.3 %collective-permute-done = bf16[128,1280]{1,0:T(8,128)(2,1)S(1)} collective-permute-done((bf16[128,1280]{1,0:T(8,128)(2,1)}, bf16[128,1280]{1,0:T(8,128)(2,1)S(1)}, u32[]{:S(2)}, u32[]{:S(2)}) %collective-permute-start) | collective-permute-done | bytes 327712 | tf_op jit(solution)/shard_map/ppermute | solution.py:232
  24.4 6.8 %collective-permute-done.8 = bf16[128,1280]{1,0:T(8,128)(2,1)S(1)} collective-permute-done((bf16[128,1280]{1,0:T(8,128)(2,1)S(1)}, bf16[128,1280]{1,0:T(8,128)(2,1)S(1)}, u32[]{:S(2)}, u32[]{:S(2)}) %collective-permute-start.8) | collective-permute-done | bytes 327712 | tf_op jit(solution)/shard_map/ppermute | solution.py:237
  33.1 4.1 %collective-permute-done.3 = bf16[128,1280]{1,0:T(8,128)(2,1)S(1)} collective-permute-done((bf16[128,1280]{1,0:T(8,128)(2,1)S(1)}, bf16[128,1280]{1,0:T(8,128)(2,1)S(1)}, u32[]{:S(2)}, u32[]{:S(2)}) %collective-permute-start.3) | collective-permute-done | bytes 327712 | tf_op jit(solution)/shard_map/ppermute | solution.py:237
  37.2 4.5 %shard_map.73.refs_0_ = f32[2,512,768]{2,1,0:T(8,128)S(1)} custom-call(s32[1]{0:T(128)} %bitcast.at_ref, bf16[256,1280]{1,0:T(8,128)(2,1)S(1)} %constant_dynamic-update-slice_fusion.near_ref, bf16[256,1280]{1,0:T(8,128)(2,1)S(1)} %collective-permute-done.5.far_ref, bf16[2,5120,384]{2,1,0:T(8,128)(2,1)} %gate_ref.7, bf16[2,5120,384]{2,1,0:T(8,128)(2,1)} %up_ref.7), custom_call_target="tpu_custom_call" | custom-call | flops 8000000000 | bytes 8000000000 | tf_op jit(solution)/shard_map/pallas_call | solution.py:163
  43.0 4.6 %shard_map.74.refs_0_ = f32[2,512,768]{2,1,0:T(8,128)S(1)} custom-call(s32[1]{0:T(128)} %bitcast.2.at_ref, bf16[256,1280]{1,0:T(8,128)(2,1)S(1)} %pad_maximum_fusion.2.near_ref, bf16[256,1280]{1,0:T(8,128)(2,1)S(1)} %collective-permute-done.11.far_ref, bf16[2,5120,384]{2,1,0:T(8,128)(2,1)} %gate_ref.7, bf16[2,5120,384]{2,1,0:T(8,128)(2,1)} %up_ref.7, ...), custom_call_target="tpu_custom_call" | custom-call | flops 8000000000 | bytes 8000000000 | tf_op jit(solution)/shard_map/pallas_call | solution.py:163
  47.6 4.6 %shard_map.75.total_ref = f32[2,512,768]{2,1,0:T(8,128)S(1)} custom-call(s32[1]{0:T(128)} %bitcast.1.at_ref, bf16[256,1280]{1,0:T(8,128)(2,1)S(1)} %pad_maximum_fusion.1.near_ref, bf16[256,1280]{1,0:T(8,128)(2,1)S(1)} %collective-permute-done.6.far_ref, bf16[2,5120,384]{2,1,0:T(8,128)(2,1)} %gate_ref.7, bf16[2,5120,384]{2,1,0:T(8,128)(2,1)} %up_ref.7, ...), custom_call_target="tpu_custom_call" | custom-call | flops 8000000000 | bytes 8000000000 | tf_op jit(solution)/shard_map/pallas_call | solution.py:163
  52.2 3.3 %shard_map.76 = (bf16[2,1280,768]{2,1,0:T(8,128)(2,1)S(1)}, bf16[2,384,1280]{2,1,0:T(8,128)(2,1)S(1)}) custom-call(s32[2]{0:T(128)S(1)} %pad_add_fusion.at_ref, bf16[2,5120,384]{2,1,0:T(8,128)(2,1)} %gate_ref.7, bf16[2,5120,384]{2,1,0:T(8,128)(2,1)} %up_ref.7, bf16[2,384,5120]{2,1,0:T(8,128)(2,1)} %down_ref.7), custom_call_target="tpu_custom_call" | custom-call | flops 8000000000 | bytes 8000000000 | tf_op jit(solution)/shard_map/pallas_call | solution.py:173
  55.5 3.5 %shard_map.77 = (bf16[512,768]{1,0:T(8,128)(2,1)S(1)}, f32[256,1280]{1,0:T(8,128)S(1)}, bf16[256,1280]{1,0:T(8,128)(2,1)S(1)}) custom-call(bf16[256,1280]{1,0:T(8,128)(2,1)S(1)} %pad_maximum_fusion.near_ref, bf16[256,1280]{1,0:T(8,128)(2,1)S(1)} %collective-permute-done.12.far_ref, f32[2,512,768]{2,1,0:T(8,128)S(1)} %shard_map.75.total_ref, ...), custom_call_target="tpu_custom_call" | custom-call | flops 8000000000 | bytes 8000000000 | tf_op jit(solution)/shard_map/pallas_call | solution.py:187
  59.6 2.7 %shard_map.78 = (f32[256,1280]{1,0:T(8,128)S(1)}, bf16[256,1280]{1,0:T(8,128)(2,1)S(1)}) custom-call(s32[1]{0:T(128)} %bitcast.1.at_ref, bf16[512,768]{1,0:T(8,128)(2,1)S(1)} %get-tuple-element.44.hidden_ref, bf16[2,384,5120]{2,1,0:T(8,128)(2,1)} %down_ref.7), custom_call_target="tpu_custom_call" | custom-call | flops 8000000000 | bytes 8000000000 | tf_op jit(solution)/shard_map/pallas_call | solution.py:196
  63.2 2.9 %shard_map.80 = (f32[256,1280]{1,0:T(8,128)S(1)}, bf16[256,1280]{1,0:T(8,128)(2,1)S(1)}) custom-call(s32[1]{0:T(128)} %bitcast.2.at_ref, bf16[512,768]{1,0:T(8,128)(2,1)S(1)} %get-tuple-element.44.hidden_ref, bf16[2,384,5120]{2,1,0:T(8,128)(2,1)} %down_ref.7), custom_call_target="tpu_custom_call" | custom-call | flops 8000000000 | bytes 8000000000 | tf_op jit(solution)/shard_map/pallas_call | solution.py:196
  68.1 2.7 %shard_map.79 = (f32[256,1280]{1,0:T(8,128)S(1)}, bf16[256,1280]{1,0:T(8,128)(2,1)S(1)}) custom-call(s32[1]{0:T(128)} %bitcast.at_ref, bf16[512,768]{1,0:T(8,128)(2,1)S(1)} %get-tuple-element.44.hidden_ref, bf16[2,384,5120]{2,1,0:T(8,128)(2,1)} %down_ref.7), custom_call_target="tpu_custom_call" | custom-call | flops 8000000000 | bytes 8000000000 | tf_op jit(solution)/shard_map/pallas_call | solution.py:196
  70.9 2.3 %collective-permute-done.18 = bf16[128,1280]{1,0:T(8,128)(2,1)S(1)} collective-permute-done((bf16[128,1280]{1,0:T(8,128)(2,1)S(1)}, bf16[128,1280]{1,0:T(8,128)(2,1)S(1)}, u32[]{:S(2)}, u32[]{:S(2)}) %collective-permute-start.18) | collective-permute-done | bytes 327712 | tf_op jit(solution)/shard_map/ppermute | solution.py:237
  73.2 1.8 %collective-permute-start.19 = (bf16[128,1280]{1,0:T(8,128)(2,1)S(1)}, bf16[128,1280]{1,0:T(8,128)(2,1)S(1)}, u32[]{:S(2)}, u32[]{:S(2)}) collective-permute-start(bf16[128,1280]{1,0:T(8,128)(2,1)S(1)} %add_convert_fusion.1), channel_id=1, source_target_pairs={{0,1},{1,0},{2,3},{3,2},{4,5},{5,4},{6,7},{7,6},{8,9},{9,8},{10,11... | collective-permute-start | bytes 983048 | tf_op jit(solution)/shard_map/ppermute | solution.py:232
  77.6 2.6 %collective-permute-done.17 = bf16[128,1280]{1,0:T(8,128)(2,1)S(1)} collective-permute-done((bf16[128,1280]{1,0:T(8,128)(2,1)S(1)}, bf16[128,1280]{1,0:T(8,128)(2,1)S(1)}, u32[]{:S(2)}, u32[]{:S(2)}) %collective-permute-start.17) | collective-permute-done | bytes 327712 | tf_op jit(solution)/shard_map/ppermute | solution.py:237
  80.2 2.1 %collective-permute-done.19 = bf16[128,1280]{1,0:T(8,128)(2,1)S(1)} collective-permute-done((bf16[128,1280]{1,0:T(8,128)(2,1)S(1)}, bf16[128,1280]{1,0:T(8,128)(2,1)S(1)}, u32[]{:S(2)}, u32[]{:S(2)}) %collective-permute-start.19) | collective-permute-done | bytes 327712 | tf_op jit(solution)/shard_map/ppermute | solution.py:232
  82.4 3.3 %collective-permute-start.20 = (bf16[128,1280]{1,0:T(8,128)(2,1)S(1)}, bf16[128,1280]{1,0:T(8,128)(2,1)S(1)}, u32[]{:S(2)}, u32[]{:S(2)}) collective-permute-start(bf16[128,1280]{1,0:T(8,128)(2,1)S(1)} %add_convert_fusion), channel_id=1, source_target_pairs={{0,2},{1,3},{2,0},{3,1},{4,6},{5,7},{6,4},{7,5},{8,10},{9,11},{10,... | collective-permute-start | bytes 983048 | tf_op jit(solution)/shard_map/ppermute | solution.py:232
  87.3 1.8 %collective-permute-start.23 = (bf16[128,1280]{1,0:T(8,128)(2,1)S(1)}, bf16[128,1280]{1,0:T(8,128)(2,1)S(1)}, u32[]{:S(2)}, u32[]{:S(2)}) collective-permute-start(bf16[128,1280]{1,0:T(8,128)(2,1)S(1)} %fusion.4), channel_id=1, source_target_pairs={{0,1},{1,0},{2,3},{3,2},{4,5},{5,4},{6,7},{7,6},{8,9},{9,8},{10,11... | collective-permute-start | bytes 983048 | tf_op jit(solution)/shard_map/ppermute | solution.py:232
  89.1 4.7 %collective-permute-done.16 = bf16[128,1280]{1,0:T(8,128)(2,1)S(1)} collective-permute-done((bf16[128,1280]{1,0:T(8,128)(2,1)S(1)}, bf16[128,1280]{1,0:T(8,128)(2,1)S(1)}, u32[]{:S(2)}, u32[]{:S(2)}) %collective-permute-start.16) | collective-permute-done | bytes 327712 | tf_op jit(solution)/shard_map/ppermute | solution.py:237
  93.8 5.6 %collective-permute-done.20 = bf16[128,1280]{1,0:T(8,128)(2,1)S(1)} collective-permute-done((bf16[128,1280]{1,0:T(8,128)(2,1)S(1)}, bf16[128,1280]{1,0:T(8,128)(2,1)S(1)}, u32[]{:S(2)}, u32[]{:S(2)}) %collective-permute-start.20) | collective-permute-done | bytes 327712 | tf_op jit(solution)/shard_map/ppermute | solution.py:232
  99.4 2.9 %collective-permute-done.23 = bf16[128,1280]{1,0:T(8,128)(2,1)S(1)} collective-permute-done((bf16[128,1280]{1,0:T(8,128)(2,1)S(1)}, bf16[128,1280]{1,0:T(8,128)(2,1)S(1)}, u32[]{:S(2)}, u32[]{:S(2)}) %collective-permute-start.23) | collective-permute-done | bytes 327712 | tf_op jit(solution)/shard_map/ppermute | solution.py:232
  (57 shorter events, 19.5 us)
Async XLA Ops:
  0.0 21.0 %collective-permute-start.4 = (bf16[128,1280]{1,0:T(8,128)(2,1)}, bf16[128,1280]{1,0:T(8,128)(2,1)S(1)}, u32[]{:S(2)}, u32[]{:S(2)}) collective-permute-start(bf16[128,1280]{1,0:T(8,128)(2,1)} %param.7), channel_id=1, source_target_pairs={{0,8},{4,12},{8,0},{12,4},{1,9},{5,13},{9,1},{13,5},{2,10},{6,14},... | collective-permute-start | bytes 983048 | tf_op jit(solution)/shard_map/ppermute | solution.py:237
  2.9 17.4 %collective-permute-start = (bf16[128,1280]{1,0:T(8,128)(2,1)}, bf16[128,1280]{1,0:T(8,128)(2,1)S(1)}, u32[]{:S(2)}, u32[]{:S(2)}) collective-permute-start(bf16[128,1280]{1,0:T(8,128)(2,1)} %param.7), channel_id=1, source_target_pairs={{0,2},{1,3},{2,0},{3,1},{4,6},{5,7},{6,4},{7,5},{8,10},{9,11},{10,... | collective-permute-start | bytes 983048 | tf_op jit(solution)/shard_map/ppermute | solution.py:232
  5.5 15.0 %collective-permute-start.7 = (bf16[128,1280]{1,0:T(8,128)(2,1)}, bf16[128,1280]{1,0:T(8,128)(2,1)S(1)}, u32[]{:S(2)}, u32[]{:S(2)}) collective-permute-start(bf16[128,1280]{1,0:T(8,128)(2,1)} %param.7), channel_id=1, source_target_pairs={{0,1},{1,0},{2,3},{3,2},{4,5},{5,4},{6,7},{7,6},{8,9},{9,8},{10,11... | collective-permute-start | bytes 983048 | tf_op jit(solution)/shard_map/ppermute | solution.py:232
  9.4 3.7 %collective-permute-start.9 = (f32[1,8,128]{2,1,0:T(8,128)S(1)}, f32[1,8,128]{2,1,0:T(8,128)S(1)}, u32[]{:S(2)}, u32[]{:S(2)}) collective-permute-start(f32[1,8,128]{2,1,0:T(8,128)S(1)} %fusion.3), channel_id=1, source_target_pairs={{0,8},{4,12},{8,0},{12,4},{1,9},{5,13},{9,1},{13,5},{2,10},{6,14},... | collective-permute-start | bytes 12296 | tf_op jit(solution)/shard_map/ppermute | solution.py:237
  13.0 11.2 %collective-permute-start.10 = (f32[2,8,128]{2,1,0:T(8,128)S(1)}, f32[2,8,128]{2,1,0:T(8,128)S(1)}, u32[]{:S(2)}, u32[]{:S(2)}) collective-permute-start(f32[2,8,128]{2,1,0:T(8,128)S(1)} %pad_maximum_fusion.3), channel_id=1, source_target_pairs={{0,4},{4,0},{8,12},{12,8},{1,5},{5,1},{9,13},{13,9},{2,6},{6,2},{1... | collective-permute-start | bytes 24584 | tf_op jit(solution)/shard_map/ppermute | solution.py:248
  20.5 10.7 %collective-permute-start.8 = (bf16[128,1280]{1,0:T(8,128)(2,1)S(1)}, bf16[128,1280]{1,0:T(8,128)(2,1)S(1)}, u32[]{:S(2)}, u32[]{:S(2)}) collective-permute-start(bf16[128,1280]{1,0:T(8,128)(2,1)S(1)} %collective-permute-done.7), channel_id=1, source_target_pairs={{0,8},{4,12},{8,0},{12,4},{1,9},{5,13},{9,1},{13,5},{2,10},{6,14},... | collective-permute-start | bytes 983048 | tf_op jit(solution)/shard_map/ppermute | solution.py:237
  21.1 16.2 %collective-permute-start.5 = (bf16[256,1280]{1,0:T(8,128)(2,1)S(1)}, bf16[256,1280]{1,0:T(8,128)(2,1)S(1)}, u32[]{:S(2)}, u32[]{:S(2)}) collective-permute-start(bf16[256,1280]{1,0:T(8,128)(2,1)S(1)} %constant_dynamic-update-slice_fusion.near_ref), channel_id=1, source_target_pairs={{0,4},{4,0},{8,12},{12,8},{1,5},{5,1},{9,13},{13,9},{2,6},{6,2},{1... | collective-permute-start | bytes 1966088 | tf_op jit(solution)/shard_map/ppermute | solution.py:248
  21.2 15.9 %collective-permute-start.3 = (bf16[128,1280]{1,0:T(8,128)(2,1)S(1)}, bf16[128,1280]{1,0:T(8,128)(2,1)S(1)}, u32[]{:S(2)}, u32[]{:S(2)}) collective-permute-start(bf16[128,1280]{1,0:T(8,128)(2,1)S(1)} %collective-permute-done), channel_id=1, source_target_pairs={{0,8},{4,12},{8,0},{12,4},{1,9},{5,13},{9,1},{13,5},{2,10},{6,14},... | collective-permute-start | bytes 983048 | tf_op jit(solution)/shard_map/ppermute | solution.py:237
  22.8 9.8 %collective-permute-start.1 = (bf16[128,1280]{1,0:T(8,128)(2,1)S(1)}, bf16[128,1280]{1,0:T(8,128)(2,1)S(1)}, u32[]{:S(2)}, u32[]{:S(2)}) collective-permute-start(bf16[128,1280]{1,0:T(8,128)(2,1)S(1)} %collective-permute-done), channel_id=1, source_target_pairs={{0,1},{1,0},{2,3},{3,2},{4,5},{5,4},{6,7},{7,6},{8,9},{9,8},{10,11... | collective-permute-start | bytes 983048 | tf_op jit(solution)/shard_map/ppermute | solution.py:232
  31.2 11.7 %collective-permute-start.11 = (bf16[256,1280]{1,0:T(8,128)(2,1)S(1)}, bf16[256,1280]{1,0:T(8,128)(2,1)S(1)}, u32[]{:S(2)}, u32[]{:S(2)}) collective-permute-start(bf16[256,1280]{1,0:T(8,128)(2,1)S(1)} %pad_maximum_fusion.2.near_ref), channel_id=1, source_target_pairs={{0,4},{4,0},{8,12},{12,8},{1,5},{5,1},{9,13},{13,9},{2,6},{6,2},{1... | collective-permute-start | bytes 1966088 | tf_op jit(solution)/shard_map/ppermute | solution.py:248
  32.6 10.3 %collective-permute-start.2 = (bf16[128,1280]{1,0:T(8,128)(2,1)S(1)}, bf16[128,1280]{1,0:T(8,128)(2,1)S(1)}, u32[]{:S(2)}, u32[]{:S(2)}) collective-permute-start(bf16[128,1280]{1,0:T(8,128)(2,1)S(1)} %collective-permute-done.1), channel_id=1, source_target_pairs={{0,8},{4,12},{8,0},{12,4},{1,9},{5,13},{9,1},{13,5},{2,10},{6,14},... | collective-permute-start | bytes 983048 | tf_op jit(solution)/shard_map/ppermute | solution.py:237
  41.8 5.8 %collective-permute-start.6 = (bf16[256,1280]{1,0:T(8,128)(2,1)S(1)}, bf16[256,1280]{1,0:T(8,128)(2,1)S(1)}, u32[]{:S(2)}, u32[]{:S(2)}) collective-permute-start(bf16[256,1280]{1,0:T(8,128)(2,1)S(1)} %pad_maximum_fusion.1.near_ref), channel_id=1, source_target_pairs={{0,4},{4,0},{8,12},{12,8},{1,5},{5,1},{9,13},{13,9},{2,6},{6,2},{1... | collective-permute-start | bytes 1966088 | tf_op jit(solution)/shard_map/ppermute | solution.py:248
  52.1 3.4 %collective-permute-start.12 = (bf16[256,1280]{1,0:T(8,128)(2,1)S(1)}, bf16[256,1280]{1,0:T(8,128)(2,1)S(1)}, u32[]{:S(2)}, u32[]{:S(2)}) collective-permute-start(bf16[256,1280]{1,0:T(8,128)(2,1)S(1)} %pad_maximum_fusion.near_ref), channel_id=1, source_target_pairs={{0,4},{4,0},{8,12},{12,8},{1,5},{5,1},{9,13},{13,9},{2,6},{6,2},{1... | collective-permute-start | bytes 1966088 | tf_op jit(solution)/shard_map/ppermute | solution.py:248
  59.0 3.4 %collective-permute-start.13 = (bf16[256,1280]{1,0:T(8,128)(2,1)S(1)}, bf16[256,1280]{1,0:T(8,128)(2,1)S(1)}, u32[]{:S(2)}, u32[]{:S(2)}) collective-permute-start(bf16[256,1280]{1,0:T(8,128)(2,1)S(1)} %get-tuple-element.40), channel_id=1, source_target_pairs={{0,4},{4,0},{8,12},{12,8},{1,5},{5,1},{9,13},{13,9},{2,6},{6,2},{1... | collective-permute-start | bytes 1966088 | tf_op jit(solution)/shard_map/ppermute | solution.py:248
  62.3 4.0 %collective-permute-start.14 = (bf16[256,1280]{1,0:T(8,128)(2,1)S(1)}, bf16[256,1280]{1,0:T(8,128)(2,1)S(1)}, u32[]{:S(2)}, u32[]{:S(2)}) collective-permute-start(bf16[256,1280]{1,0:T(8,128)(2,1)S(1)} %get-tuple-element.43), channel_id=1, source_target_pairs={{0,4},{4,0},{8,12},{12,8},{1,5},{5,1},{9,13},{13,9},{2,6},{6,2},{1... | collective-permute-start | bytes 1966088 | tf_op jit(solution)/shard_map/ppermute | solution.py:248
  62.6 10.6 %collective-permute-start.18 = (bf16[128,1280]{1,0:T(8,128)(2,1)S(1)}, bf16[128,1280]{1,0:T(8,128)(2,1)S(1)}, u32[]{:S(2)}, u32[]{:S(2)}) collective-permute-start(bf16[128,1280]{1,0:T(8,128)(2,1)S(1)} %slice.67), channel_id=1, source_target_pairs={{0,8},{4,12},{8,0},{12,4},{1,9},{5,13},{9,1},{13,5},{2,10},{6,14},... | collective-permute-start | bytes 983048 | tf_op jit(solution)/shard_map/ppermute | solution.py:237
  66.1 9.0 %collective-permute-start.21 = (bf16[256,1280]{1,0:T(8,128)(2,1)S(1)}, bf16[256,1280]{1,0:T(8,128)(2,1)S(1)}, u32[]{:S(2)}, u32[]{:S(2)}) collective-permute-start(bf16[256,1280]{1,0:T(8,128)(2,1)S(1)} %get-tuple-element.50), channel_id=1, source_target_pairs={{0,4},{4,0},{8,12},{12,8},{1,5},{5,1},{9,13},{13,9},{2,6},{6,2},{1... | collective-permute-start | bytes 1966088 | tf_op jit(solution)/shard_map/ppermute | solution.py:248
  66.5 13.7 %collective-permute-start.17 = (bf16[128,1280]{1,0:T(8,128)(2,1)S(1)}, bf16[128,1280]{1,0:T(8,128)(2,1)S(1)}, u32[]{:S(2)}, u32[]{:S(2)}) collective-permute-start(bf16[128,1280]{1,0:T(8,128)(2,1)S(1)} %slice.68), channel_id=1, source_target_pairs={{0,8},{4,12},{8,0},{12,4},{1,9},{5,13},{9,1},{13,5},{2,10},{6,14},... | collective-permute-start | bytes 983048 | tf_op jit(solution)/shard_map/ppermute | solution.py:237
  70.8 5.0 %collective-permute-start.15 = (bf16[256,1280]{1,0:T(8,128)(2,1)S(1)}, bf16[256,1280]{1,0:T(8,128)(2,1)S(1)}, u32[]{:S(2)}, u32[]{:S(2)}) collective-permute-start(bf16[256,1280]{1,0:T(8,128)(2,1)S(1)} %get-tuple-element.46), channel_id=1, source_target_pairs={{0,4},{4,0},{8,12},{12,8},{1,5},{5,1},{9,13},{13,9},{2,6},{6,2},{1... | collective-permute-start | bytes 1966088 | tf_op jit(solution)/shard_map/ppermute | solution.py:248
  73.2 9.0 %collective-permute-start.19 = (bf16[128,1280]{1,0:T(8,128)(2,1)S(1)}, bf16[128,1280]{1,0:T(8,128)(2,1)S(1)}, u32[]{:S(2)}, u32[]{:S(2)}) collective-permute-start(bf16[128,1280]{1,0:T(8,128)(2,1)S(1)} %add_convert_fusion.1), channel_id=1, source_target_pairs={{0,1},{1,0},{2,3},{3,2},{4,5},{5,4},{6,7},{7,6},{8,9},{9,8},{10,11... | collective-permute-start | bytes 983048 | tf_op jit(solution)/shard_map/ppermute | solution.py:232
  75.2 12.0 %collective-permute-start.22 = (bf16[128,1280]{1,0:T(8,128)(2,1)S(1)}, bf16[128,1280]{1,0:T(8,128)(2,1)S(1)}, u32[]{:S(2)}, u32[]{:S(2)}) collective-permute-start(bf16[128,1280]{1,0:T(8,128)(2,1)S(1)} %slice.66), channel_id=1, source_target_pairs={{0,8},{4,12},{8,0},{12,4},{1,9},{5,13},{9,1},{13,5},{2,10},{6,14},... | collective-permute-start | bytes 983048 | tf_op jit(solution)/shard_map/ppermute | solution.py:237
  76.0 17.8 %collective-permute-start.16 = (bf16[128,1280]{1,0:T(8,128)(2,1)S(1)}, bf16[128,1280]{1,0:T(8,128)(2,1)S(1)}, u32[]{:S(2)}, u32[]{:S(2)}) collective-permute-start(bf16[128,1280]{1,0:T(8,128)(2,1)S(1)} %slice.69), channel_id=1, source_target_pairs={{0,8},{4,12},{8,0},{12,4},{1,9},{5,13},{9,1},{13,5},{2,10},{6,14},... | collective-permute-start | bytes 983048 | tf_op jit(solution)/shard_map/ppermute | solution.py:237
  82.4 17.0 %collective-permute-start.20 = (bf16[128,1280]{1,0:T(8,128)(2,1)S(1)}, bf16[128,1280]{1,0:T(8,128)(2,1)S(1)}, u32[]{:S(2)}, u32[]{:S(2)}) collective-permute-start(bf16[128,1280]{1,0:T(8,128)(2,1)S(1)} %add_convert_fusion), channel_id=1, source_target_pairs={{0,2},{1,3},{2,0},{3,1},{4,6},{5,7},{6,4},{7,5},{8,10},{9,11},{10,... | collective-permute-start | bytes 983048 | tf_op jit(solution)/shard_map/ppermute | solution.py:232
  87.3 15.1 %collective-permute-start.23 = (bf16[128,1280]{1,0:T(8,128)(2,1)S(1)}, bf16[128,1280]{1,0:T(8,128)(2,1)S(1)}, u32[]{:S(2)}, u32[]{:S(2)}) collective-permute-start(bf16[128,1280]{1,0:T(8,128)(2,1)S(1)} %fusion.4), channel_id=1, source_target_pairs={{0,1},{1,0},{2,3},{3,2},{4,5},{5,4},{6,7},{7,6},{8,9},{9,8},{10,11... | collective-permute-start | bytes 983048 | tf_op jit(solution)/shard_map/ppermute | solution.py:232

commit v3 on v2

--- a/solution.py
+++ b/solution.py
@@ -7,7 +7,7 @@
 from jax.experimental.pallas import tpu as pltpu
 from jax.sharding import PartitionSpec as P
 
-VMEM_LIMIT = 16 * 1024 * 1024
+VMEM_LIMIT = 20 * 1024 * 1024
 COST = 8000000000
 VMEM = pl.BlockSpec(memory_space=pltpu.VMEM)
 HBM = pl.BlockSpec(memory_space=pltpu.HBM)
@@ -82,17 +82,32 @@
     return parts[0] if len(parts) == 1 else jnp.concatenate(parts, axis=1)
 
 
-def gate_up_kernel(first, at_ref, near_ref, far_ref, gate_ref, up_ref, *refs):
-    total_ref, refs = (None, refs) if first else (refs[0], refs[1:])
-    out_ref, part_refs, sems = refs[0], refs[1:-1], refs[-1]
-    loads = load_parts([gate_ref, up_ref], part_refs, sems, at_ref[0])
-    for copies in loads:
+def gate_up_kernel(first, loads_down, at_ref, near_ref, far_ref, gate_ref, up_ref, *refs):
+    refs = list(refs)
+    per = 1 if gate_ref.shape[2] % 128 == 0 else 2
+    down_ref = refs.pop(0) if loads_down else None
+    total_ref = None if first else refs.pop(0)
+    part_refs = None if first else [refs.pop(0) for _ in range(per)]
+    out_ref = refs.pop(0)
+    next_refs = [refs.pop(0) for _ in range(per)]
+    down_part = refs.pop(0) if loads_down else None
+    own_loads = []
+    if first:
+        part_refs = [refs.pop(0) for _ in range(per)]
+        own_loads = load_parts([gate_ref, up_ref], part_refs, refs.pop(0), at_ref[0])
+    next_loads = load_parts([gate_ref, up_ref], next_refs, refs.pop(0), at_ref[1])
+    if loads_down:
+        next_loads.append(load_down(down_ref, down_part, refs.pop(0), at_ref[1]))
+    for copies in own_loads + next_loads:
         start(copies)
     rows = jnp.concatenate([near_ref[...], far_ref[...]], axis=0)
-    for index, copies in enumerate(loads):
-        wait(copies)
+    for index in range(out_ref.shape[0]):
+        if first:
+            wait(own_loads[index])
         value = products(rows, part_refs, index)
         out_ref[index] = value if first else value + total_ref[index]
+    for copies in next_loads:
+        wait(copies)
 
 
 def down_product(value, part_ref, keep_ref, send_ref):
@@ -108,16 +123,6 @@
     keep_ref[...] = result[:half]
 
 
-def last_load_kernel(at_ref, gate_ref, up_ref, down_ref, *refs):
-    part_refs, (down_part, sems, down_sems) = refs[:-3], refs[-3:]
-    loads = load_parts([gate_ref, up_ref], part_refs, sems, at_ref[0])
-    loads.append(load_down(down_ref, down_part, down_sems, at_ref[1]))
-    for copies in loads:
-        start(copies)
-    for copies in loads:
-        wait(copies)
-
-
 def hidden_kernel(near_ref, far_ref, total_ref, weight_ref, *refs):
     part_refs, (down_part, out_ref, keep_ref, send_ref) = refs[:-4], refs[-4:]
     width = total_ref.shape[2] // 2
@@ -156,29 +161,31 @@
     ]
 
 
-def gate_up(at, near, far, w_gate, w_up, total):
+def gate_up(at, near, far, w_gate, w_up, total, parts, w_down):
     local_count, _, width = w_gate.shape
     half, depth = near.shape
-    totals = [] if total is None else [total]
-    return call(
-        functools.partial(gate_up_kernel, total is None),
-        jax.ShapeDtypeStruct((local_count, 2 * half, 2 * width), jnp.float32),
-        [SMEM, VMEM, VMEM, HBM, HBM] + [VMEM] * len(totals),
-        scratch_shapes=part_scratch(w_gate, depth) + [pltpu.SemaphoreType.DMA((2 * local_count,))],
-    )(at, near, far, in_hbm(w_gate), in_hbm(w_up), *totals)
-
-
-def last_load(at, w_gate, w_up, w_down, depth):
-    local_count = w_gate.shape[0]
-    return call(
-        last_load_kernel,
-        part_scratch(w_gate, depth) + [down_scratch(w_down, depth)],
-        [SMEM, HBM, HBM, HBM],
-        scratch_shapes=[
-            pltpu.SemaphoreType.DMA((2 * local_count,)),
-            pltpu.SemaphoreType.DMA((local_count,)),
-        ],
-    )(at, in_hbm(w_gate), in_hbm(w_up), in_hbm(w_down))
+    first, loads_down = total is None, w_down is not None
+    shapes = [jax.ShapeDtypeStruct((local_count, 2 * half, 2 * width), jnp.float32)]
+    shapes += part_scratch(w_gate, depth)
+    scratch = [pltpu.SemaphoreType.DMA((2 * local_count,))]
+    if first:
+        scratch = part_scratch(w_gate, depth) + scratch + scratch
+    more, specs = [], []
+    if loads_down:
+        shapes.append(down_scratch(w_down, depth))
+        scratch.append(pltpu.SemaphoreType.DMA((local_count,)))
+        more.append(in_hbm(w_down))
+        specs.append(HBM)
+    if not first:
+        more += [total, *map(in_vmem, parts)]
+        specs += [VMEM] * (1 + len(parts))
+    total, *parts = call(
+        functools.partial(gate_up_kernel, first, loads_down),
+        shapes,
+        [SMEM, VMEM, VMEM, HBM, HBM] + specs,
+        scratch_shapes=scratch,
+    )(at, near, far, in_hbm(w_gate), in_hbm(w_up), *more)
+    return total, parts
 
 
 def hidden(near, far, total, weight, parts):
@@ -266,7 +273,7 @@
     def both_chips(piece):
         return jnp.concatenate([over_chips(piece, c) for c in range(chip_count)], axis=0)
 
-    gates = {'q1': ['p2'], 'm1': ['weights'], 'm2': ['t0'], 'm3': ['t2'], 'a0': ['t2']}
+    gates = {'q1': ['p2'], 'm1': ['weights'], 'm2': ['t0']}
     last = seq_count - 1
     have = {"p0": tokens, "weights": own_weights, "w": weights}
 
@@ -278,26 +285,27 @@
             return have[name]
         kind, flip = name[0], int(name[1:])
         if kind == "p":
-            value = over_seq(get("p%d" % (flip & (flip - 1))), flip & -flip)
+            value = over_seq(get("r%d" % flip), flip & -flip)
+        elif kind == "r":
+            value = get("p%d" % (flip & (flip - 1)))
         elif kind == "q":
             value = get("p%d" % flip)
         elif kind == "n":
             value = both_chips(get("q%d" % flip))
         elif kind == "m":
             value = get("n%d" % flip)
-        elif kind == "a":
-            value = jnp.concatenate([places(last), places(last)])
-        elif kind == "l":
-            value = last_load(get("a0"), w_gate, w_up, w_down, depth)
         elif kind == "c":
             value = over_core(get("m%d" % flip))
         else:
+            before = get("t%d" % (flip - 1)) if flip else None
             pair = get("m%d" % flip), get("c%d" % flip)
-            before = get("t%d" % (flip - 1)) if flip else None
+            parts = have.get("parts")
             if flip < last:
-                value = gate_up(places(flip), *pair, w_gate, w_up, before)
+                at = jnp.concatenate([places(flip), places(flip + 1)])
+                late = w_down if flip == last - 1 else None
+                value, have["parts"] = gate_up(at, *pair, w_gate, w_up, before, parts, late)
             else:
-                value, *have["first"] = hidden(*pair, before, get("weights"), get("l0"))
+                value, *have["first"] = hidden(*pair, before, get("weights"), parts)
         for other in gates.get(name, ()):
             value, have[other] = after((value, get(other)))
         have[name] = value

time: 104 us -> 101 us (0.971)
  Pallas kernels: 28.8 us -> 27 us
  starting transfers between devices: 24.3 us -> 22.7 us
    ppermute x9, waiting for transfers between devices: 25.2 us -> 29.1 us  [over_chips(): lax.ppermute(value, 'expert', [(2 * i + c, 2 * ((i + shift) % chip_count)...]
    ppermute x6, waiting for transfers between devices: 19.4 us -> 16.3 us  [over_seq(): return lax.ppermute(value, 'seq', [(i, i ^ flip) for i in range(seq_count)])]
    pallas_call x4 -> x3, Pallas kernels: 17 us -> 15.2 us  [gate_up(): call(functools.partial(gate_up_kernel, first, loads_down), shapes, [SMEM,...]
  transfers between devices with their start and end apart: 24 -> 24, of which waited for: 14 -> 13; matrix products, arithmetic and copies ran while one was open for 4% -> 5% of each run, Pallas kernels for 20% -> 23%
where the time goes in v3:
time: 101 us
  waiting for transfers between devices  45.4 us (45%)
  Pallas kernels  27 us (27%)
  starting transfers between devices  22.7 us (22%)
  other arithmetic  4.11 us (4%)
  local copies, waits for them, and re-layouts  1.35 us (1%)
    ppermute x9, waiting for transfers between devices, over_chips(): lax.ppermute(value, 'expert', [(2 * i + c, 2 * ((i + shift) % chip_count)...  29.1 us
    ppermute x6, waiting for transfers between devices, over_seq(): return lax.ppermute(value, 'seq', [(i, i ^ flip) for i in range(seq_count)])  16.3 us
    pallas_call x3, Pallas kernels, gate_up(): call(functools.partial(gate_up_kernel, first, loads_down), shapes, [SMEM,...  15.2 us
    ppermute x6, starting transfers between devices, over_seq(): return lax.ppermute(value, 'seq', [(i, i ^ flip) for i in range(seq_count)])  11.8 us
    ppermute x9, starting transfers between devices, over_chips(): lax.ppermute(value, 'expert', [(2 * i + c, 2 * ((i + shift) % chip_count)...  9.88 us
    pallas_call x3, Pallas kernels, down(): call(down_kernel, down_shapes(value.shape[0] // 2, depth), [SMEM, VMEM, H...  8.13 us
    pallas_call x1, Pallas kernels, hidden(): call(hidden_kernel, [jax.ShapeDtypeStruct((row_count, local_count * width...  3.62 us
  transfers between devices with their start and end apart: 24, of which 13 were waited for; matrix products, arithmetic and copies ran while one was open for 5% of the time, Pallas kernels for 23%

profile of v3, /device:TPU:0, one launch (start us, length us, event | category | flops | bytes accessed | tf_op | source)
XLA Modules:
  0.0 101.0 jit_solution(15780788123463000870)
XLA Ops:
  0.0 3.0 %collective-permute-start = (bf16[128,1280]{1,0:T(8,128)(2,1)}, bf16[128,1280]{1,0:T(8,128)(2,1)S(1)}, u32[]{:S(2)}, u32[]{:S(2)}) collective-permute-start(bf16[128,1280]{1,0:T(8,128)(2,1)} %param.7), channel_id=1, source_target_pairs={{0,1},{1,0},{2,3},{3,2},{4,5},{5,4},{6,7},{7,6},{8,9},{9,8},{10,11... | collective-permute-start | bytes 983048 | tf_op jit(solution)/shard_map/ppermute | solution.py:239
  3.0 2.6 %collective-permute-start.1 = (bf16[128,1280]{1,0:T(8,128)(2,1)}, bf16[128,1280]{1,0:T(8,128)(2,1)S(1)}, u32[]{:S(2)}, u32[]{:S(2)}) collective-permute-start(bf16[128,1280]{1,0:T(8,128)(2,1)} %param.7), channel_id=1, source_target_pairs={{0,2},{1,3},{2,0},{3,1},{4,6},{5,7},{6,4},{7,5},{8,10},{9,11},{10,... | collective-permute-start | bytes 983048 | tf_op jit(solution)/shard_map/ppermute | solution.py:239
  11.1 3.7 %collective-permute-done.10 = f32[1,8,128]{2,1,0:T(8,128)S(1)} collective-permute-done((f32[1,8,128]{2,1,0:T(8,128)S(1)}, f32[1,8,128]{2,1,0:T(8,128)S(1)}, u32[]{:S(2)}, u32[]{:S(2)}) %collective-permute-start.10) | collective-permute-done | bytes 4128 | tf_op jit(solution)/shard_map/ppermute | solution.py:244
  14.9 2.9 %collective-permute-done = bf16[128,1280]{1,0:T(8,128)(2,1)S(1)} collective-permute-done((bf16[128,1280]{1,0:T(8,128)(2,1)}, bf16[128,1280]{1,0:T(8,128)(2,1)S(1)}, u32[]{:S(2)}, u32[]{:S(2)}) %collective-permute-start) | collective-permute-done | bytes 327712 | tf_op jit(solution)/shard_map/ppermute | solution.py:239
  17.8 2.6 %collective-permute-done.1 = bf16[128,1280]{1,0:T(8,128)(2,1)S(1)} collective-permute-done((bf16[128,1280]{1,0:T(8,128)(2,1)}, bf16[128,1280]{1,0:T(8,128)(2,1)S(1)}, u32[]{:S(2)}, u32[]{:S(2)}) %collective-permute-start.1) | collective-permute-done | bytes 327712 | tf_op jit(solution)/shard_map/ppermute | solution.py:239
  20.4 1.5 %collective-permute-start.9 = (bf16[128,1280]{1,0:T(8,128)(2,1)S(1)}, bf16[128,1280]{1,0:T(8,128)(2,1)S(1)}, u32[]{:S(2)}, u32[]{:S(2)}) collective-permute-start(bf16[128,1280]{1,0:T(8,128)(2,1)S(1)} %collective-permute-done), channel_id=1, source_target_pairs={{0,8},{4,12},{8,0},{12,4},{1,9},{5,13},{9,1},{13,5},{2,10},{6,14},... | collective-permute-start | bytes 983048 | tf_op jit(solution)/shard_map/ppermute | solution.py:244
  23.2 7.1 %collective-permute-done.9 = bf16[128,1280]{1,0:T(8,128)(2,1)S(1)} collective-permute-done((bf16[128,1280]{1,0:T(8,128)(2,1)S(1)}, bf16[128,1280]{1,0:T(8,128)(2,1)S(1)}, u32[]{:S(2)}, u32[]{:S(2)}) %collective-permute-start.9) | collective-permute-done | bytes 327712 | tf_op jit(solution)/shard_map/ppermute | solution.py:244
  31.8 2.2 %collective-permute-done.5 = bf16[128,1280]{1,0:T(8,128)(2,1)S(1)} collective-permute-done((bf16[128,1280]{1,0:T(8,128)(2,1)S(1)}, bf16[128,1280]{1,0:T(8,128)(2,1)S(1)}, u32[]{:S(2)}, u32[]{:S(2)}) %collective-permute-start.5) | collective-permute-done | bytes 327712 | tf_op jit(solution)/shard_map/ppermute | solution.py:244
  34.0 5.1 %shard_map.73 = (f32[2,512,768]{2,1,0:T(8,128)S(1)}, bf16[2,1280,768]{2,1,0:T(8,128)(2,1)S(1)}) custom-call(s32[2]{0:T(128)S(1)} %pad_add_fusion.1.at_ref, bf16[256,1280]{1,0:T(8,128)(2,1)S(1)} %constant_dynamic-update-slice_fusion.2.near_ref, bf16[256,1280]{1,0:T(8,128)(2,1)S(1)} %collective-permute-done.7.far_ref, bf16[2,5120,384]{2,1,0:T(8,128)(2,1)} %gate_ref.5, ...), custom_call_target="tpu_custom_call" | custom-call | flops 8000000000 | bytes 8000000000 | tf_op jit(solution)/shard_map/pallas_call | solution.py:182
  39.2 1.5 %collective-permute-done.3 = bf16[128,1280]{1,0:T(8,128)(2,1)S(1)} collective-permute-done((bf16[128,1280]{1,0:T(8,128)(2,1)S(1)}, bf16[128,1280]{1,0:T(8,128)(2,1)S(1)}, u32[]{:S(2)}, u32[]{:S(2)}) %collective-permute-start.3) | collective-permute-done | bytes 327712 | tf_op jit(solution)/shard_map/ppermute | solution.py:244
  40.9 4.7 %shard_map.74 = (f32[2,512,768]{2,1,0:T(8,128)S(1)}, bf16[2,1280,768]{2,1,0:T(8,128)(2,1)S(1)}) custom-call(s32[2]{0:T(128)S(1)} %pad_add_fusion.2.at_ref, bf16[256,1280]{1,0:T(8,128)(2,1)S(1)} %pad_maximum_fusion.1.near_ref, bf16[256,1280]{1,0:T(8,128)(2,1)S(1)} %collective-permute-done.12.far_ref, bf16[2,5120,384]{2,1,0:T(8,128)(2,1)} %gate_ref.5, ...), custom_call_target="tpu_custom_call" | custom-call | flops 8000000000 | bytes 8000000000 | tf_op jit(solution)/shard_map/pallas_call | solution.py:182
  45.7 5.4 %shard_map.75 = (f32[2,512,768]{2,1,0:T(8,128)S(1)}, bf16[2,1280,768]{2,1,0:T(8,128)(2,1)S(1)}, bf16[2,384,1280]{2,1,0:T(8,128)(2,1)S(1)}) custom-call(s32[2]{0:T(128)S(1)} %pad_add_fusion.at_ref, bf16[256,1280]{1,0:T(8,128)(2,1)S(1)} %pad_maximum_fusion.near_ref, bf16[256,1280]{1,0:T(8,128)(2,1)S(1)} %collective-permute-done.8.far_ref, ...), custom_call_target="tpu_custom_call" | custom-call | flops 8000000000 | bytes 8000000000 | tf_op jit(solution)/shard_map/pallas_call | solution.py:182
  51.0 3.6 %shard_map.76 = (bf16[512,768]{1,0:T(8,128)(2,1)S(1)}, f32[256,1280]{1,0:T(8,128)S(1)}, bf16[256,1280]{1,0:T(8,128)(2,1)S(1)}) custom-call(bf16[256,1280]{1,0:T(8,128)(2,1)S(1)} %constant_dynamic-update-slice_fusion.near_ref, bf16[256,1280]{1,0:T(8,128)(2,1)S(1)} %collective-permute-done.4.far_ref, f32[2,512,768]{2,1,0:T(8,128)S(1)} %get-tuple-element.38.total_ref, ...), custom_call_target="tpu_custom_call" | custom-call | flops 8000000000 | bytes 8000000000 | tf_op jit(solution)/shard_map/pallas_call | solution.py:194
  55.2 2.7 %shard_map.77 = (f32[256,1280]{1,0:T(8,128)S(1)}, bf16[256,1280]{1,0:T(8,128)(2,1)S(1)}) custom-call(s32[1]{0:T(128)} %bitcast.1.at_ref, bf16[512,768]{1,0:T(8,128)(2,1)S(1)} %get-tuple-element.48.hidden_ref, bf16[2,384,5120]{2,1,0:T(8,128)(2,1)} %down_ref.5), custom_call_target="tpu_custom_call" | custom-call | flops 8000000000 | bytes 8000000000 | tf_op jit(solution)/shard_map/pallas_call | solution.py:203
  59.6 2.7 %shard_map.79 = (f32[256,1280]{1,0:T(8,128)S(1)}, bf16[256,1280]{1,0:T(8,128)(2,1)S(1)}) custom-call(s32[1]{0:T(128)} %bitcast.3.at_ref, bf16[512,768]{1,0:T(8,128)(2,1)S(1)} %get-tuple-element.48.hidden_ref, bf16[2,384,5120]{2,1,0:T(8,128)(2,1)} %down_ref.5), custom_call_target="tpu_custom_call" | custom-call | flops 8000000000 | bytes 8000000000 | tf_op jit(solution)/shard_map/pallas_call | solution.py:203
  63.3 5.5 %collective-permute-done.18 = bf16[128,1280]{1,0:T(8,128)(2,1)S(1)} collective-permute-done((bf16[128,1280]{1,0:T(8,128)(2,1)S(1)}, bf16[128,1280]{1,0:T(8,128)(2,1)S(1)}, u32[]{:S(2)}, u32[]{:S(2)}) %collective-permute-start.18) | collective-permute-done | bytes 327712 | tf_op jit(solution)/shard_map/ppermute | solution.py:244
  68.8 3.1 %collective-permute-start.19 = (bf16[128,1280]{1,0:T(8,128)(2,1)S(1)}, bf16[128,1280]{1,0:T(8,128)(2,1)S(1)}, u32[]{:S(2)}, u32[]{:S(2)}) collective-permute-start(bf16[128,1280]{1,0:T(8,128)(2,1)S(1)} %add_convert_fusion.1), channel_id=1, source_target_pairs={{0,1},{1,0},{2,3},{3,2},{4,5},{5,4},{6,7},{7,6},{8,9},{9,8},{10,11... | collective-permute-start | bytes 983048 | tf_op jit(solution)/shard_map/ppermute | solution.py:239
  71.9 2.7 %shard_map.78 = (f32[256,1280]{1,0:T(8,128)S(1)}, bf16[256,1280]{1,0:T(8,128)(2,1)S(1)}) custom-call(s32[1]{0:T(128)} %bitcast.at_ref, bf16[512,768]{1,0:T(8,128)(2,1)S(1)} %get-tuple-element.48.hidden_ref, bf16[2,384,5120]{2,1,0:T(8,128)(2,1)} %down_ref.5), custom_call_target="tpu_custom_call" | custom-call | flops 8000000000 | bytes 8000000000 | tf_op jit(solution)/shard_map/pallas_call | solution.py:203
  75.4 2.9 %collective-permute-done.19 = bf16[128,1280]{1,0:T(8,128)(2,1)S(1)} collective-permute-done((bf16[128,1280]{1,0:T(8,128)(2,1)S(1)}, bf16[128,1280]{1,0:T(8,128)(2,1)S(1)}, u32[]{:S(2)}, u32[]{:S(2)}) %collective-permute-start.19) | collective-permute-done | bytes 327712 | tf_op jit(solution)/shard_map/ppermute | solution.py:239
  78.4 1.7 %collective-permute-start.20 = (bf16[128,1280]{1,0:T(8,128)(2,1)S(1)}, bf16[128,1280]{1,0:T(8,128)(2,1)S(1)}, u32[]{:S(2)}, u32[]{:S(2)}) collective-permute-start(bf16[128,1280]{1,0:T(8,128)(2,1)S(1)} %add_convert_fusion), channel_id=1, source_target_pairs={{0,2},{1,3},{2,0},{3,1},{4,6},{5,7},{6,4},{7,5},{8,10},{9,11},{10,... | collective-permute-start | bytes 983048 | tf_op jit(solution)/shard_map/ppermute | solution.py:239
  80.3 1.6 %collective-permute-start.22 = (bf16[128,1280]{1,0:T(8,128)(2,1)S(1)}, bf16[128,1280]{1,0:T(8,128)(2,1)S(1)}, u32[]{:S(2)}, u32[]{:S(2)}) collective-permute-start(bf16[128,1280]{1,0:T(8,128)(2,1)S(1)} %slice.66), channel_id=1, source_target_pairs={{0,8},{4,12},{8,0},{12,4},{1,9},{5,13},{9,1},{13,5},{2,10},{6,14},... | collective-permute-start | bytes 983048 | tf_op jit(solution)/shard_map/ppermute | solution.py:244
  82.6 8.2 %collective-permute-done.22 = bf16[128,1280]{1,0:T(8,128)(2,1)S(1)} collective-permute-done((bf16[128,1280]{1,0:T(8,128)(2,1)S(1)}, bf16[128,1280]{1,0:T(8,128)(2,1)S(1)}, u32[]{:S(2)}, u32[]{:S(2)}) %collective-permute-start.22) | collective-permute-done | bytes 327712 | tf_op jit(solution)/shard_map/ppermute | solution.py:244
  91.9 2.1 %collective-permute-done.20 = bf16[128,1280]{1,0:T(8,128)(2,1)S(1)} collective-permute-done((bf16[128,1280]{1,0:T(8,128)(2,1)S(1)}, bf16[128,1280]{1,0:T(8,128)(2,1)S(1)}, u32[]{:S(2)}, u32[]{:S(2)}) %collective-permute-start.20) | collective-permute-done | bytes 327712 | tf_op jit(solution)/shard_map/ppermute | solution.py:239
  94.3 5.7 %collective-permute-done.23 = bf16[128,1280]{1,0:T(8,128)(2,1)S(1)} collective-permute-done((bf16[128,1280]{1,0:T(8,128)(2,1)S(1)}, bf16[128,1280]{1,0:T(8,128)(2,1)S(1)}, u32[]{:S(2)}, u32[]{:S(2)}) %collective-permute-start.23) | collective-permute-done | bytes 327712 | tf_op jit(solution)/shard_map/ppermute | solution.py:239
  (59 shorter events, 15.9 us)
Async XLA Ops:
  0.0 17.8 %collective-permute-start = (bf16[128,1280]{1,0:T(8,128)(2,1)}, bf16[128,1280]{1,0:T(8,128)(2,1)S(1)}, u32[]{:S(2)}, u32[]{:S(2)}) collective-permute-start(bf16[128,1280]{1,0:T(8,128)(2,1)} %param.7), channel_id=1, source_target_pairs={{0,1},{1,0},{2,3},{3,2},{4,5},{5,4},{6,7},{7,6},{8,9},{9,8},{10,11... | collective-permute-start | bytes 983048 | tf_op jit(solution)/shard_map/ppermute | solution.py:239
  3.0 17.4 %collective-permute-start.1 = (bf16[128,1280]{1,0:T(8,128)(2,1)}, bf16[128,1280]{1,0:T(8,128)(2,1)S(1)}, u32[]{:S(2)}, u32[]{:S(2)}) collective-permute-start(bf16[128,1280]{1,0:T(8,128)(2,1)} %param.7), channel_id=1, source_target_pairs={{0,2},{1,3},{2,0},{3,1},{4,6},{5,7},{6,4},{7,5},{8,10},{9,11},{10,... | collective-permute-start | bytes 983048 | tf_op jit(solution)/shard_map/ppermute | solution.py:239
  5.6 17.5 %collective-permute-start.6 = (bf16[128,1280]{1,0:T(8,128)(2,1)}, bf16[128,1280]{1,0:T(8,128)(2,1)S(1)}, u32[]{:S(2)}, u32[]{:S(2)}) collective-permute-start(bf16[128,1280]{1,0:T(8,128)(2,1)} %param.7), channel_id=1, source_target_pairs={{0,8},{4,12},{8,0},{12,4},{1,9},{5,13},{9,1},{13,5},{2,10},{6,14},... | collective-permute-start | bytes 983048 | tf_op jit(solution)/shard_map/ppermute | solution.py:244
  9.4 5.4 %collective-permute-start.10 = (f32[1,8,128]{2,1,0:T(8,128)S(1)}, f32[1,8,128]{2,1,0:T(8,128)S(1)}, u32[]{:S(2)}, u32[]{:S(2)}) collective-permute-start(f32[1,8,128]{2,1,0:T(8,128)S(1)} %fusion.3), channel_id=1, source_target_pairs={{0,8},{4,12},{8,0},{12,4},{1,9},{5,13},{9,1},{13,5},{2,10},{6,14},... | collective-permute-start | bytes 12296 | tf_op jit(solution)/shard_map/ppermute | solution.py:244
  14.8 7.1 %collective-permute-start.11 = (f32[2,8,128]{2,1,0:T(8,128)S(1)}, f32[2,8,128]{2,1,0:T(8,128)S(1)}, u32[]{:S(2)}, u32[]{:S(2)}) collective-permute-start(f32[2,8,128]{2,1,0:T(8,128)S(1)} %pad_maximum_fusion.2), channel_id=1, source_target_pairs={{0,4},{4,0},{8,12},{12,8},{1,5},{5,1},{9,13},{13,9},{2,6},{6,2},{1... | collective-permute-start | bytes 24584 | tf_op jit(solution)/shard_map/ppermute | solution.py:255
  20.4 9.9 %collective-permute-start.9 = (bf16[128,1280]{1,0:T(8,128)(2,1)S(1)}, bf16[128,1280]{1,0:T(8,128)(2,1)S(1)}, u32[]{:S(2)}, u32[]{:S(2)}) collective-permute-start(bf16[128,1280]{1,0:T(8,128)(2,1)S(1)} %collective-permute-done), channel_id=1, source_target_pairs={{0,8},{4,12},{8,0},{12,4},{1,9},{5,13},{9,1},{13,5},{2,10},{6,14},... | collective-permute-start | bytes 983048 | tf_op jit(solution)/shard_map/ppermute | solution.py:244
  22.0 11.9 %collective-permute-start.5 = (bf16[128,1280]{1,0:T(8,128)(2,1)S(1)}, bf16[128,1280]{1,0:T(8,128)(2,1)S(1)}, u32[]{:S(2)}, u32[]{:S(2)}) collective-permute-start(bf16[128,1280]{1,0:T(8,128)(2,1)S(1)} %collective-permute-done.1), channel_id=1, source_target_pairs={{0,8},{4,12},{8,0},{12,4},{1,9},{5,13},{9,1},{13,5},{2,10},{6,14},... | collective-permute-start | bytes 983048 | tf_op jit(solution)/shard_map/ppermute | solution.py:244
  22.6 7.7 %collective-permute-start.2 = (bf16[128,1280]{1,0:T(8,128)(2,1)S(1)}, bf16[128,1280]{1,0:T(8,128)(2,1)S(1)}, u32[]{:S(2)}, u32[]{:S(2)}) collective-permute-start(bf16[128,1280]{1,0:T(8,128)(2,1)S(1)} %collective-permute-done.1), channel_id=1, source_target_pairs={{0,1},{1,0},{2,3},{3,2},{4,5},{5,4},{6,7},{7,6},{8,9},{9,8},{10,11... | collective-permute-start | bytes 983048 | tf_op jit(solution)/shard_map/ppermute | solution.py:239
  23.1 10.9 %collective-permute-start.7 = (bf16[256,1280]{1,0:T(8,128)(2,1)S(1)}, bf16[256,1280]{1,0:T(8,128)(2,1)S(1)}, u32[]{:S(2)}, u32[]{:S(2)}) collective-permute-start(bf16[256,1280]{1,0:T(8,128)(2,1)S(1)} %constant_dynamic-update-slice_fusion.2.near_ref), channel_id=1, source_target_pairs={{0,4},{4,0},{8,12},{12,8},{1,5},{5,1},{9,13},{13,9},{2,6},{6,2},{1... | collective-permute-start | bytes 1966088 | tf_op jit(solution)/shard_map/ppermute | solution.py:255
  30.3 10.6 %collective-permute-start.12 = (bf16[256,1280]{1,0:T(8,128)(2,1)S(1)}, bf16[256,1280]{1,0:T(8,128)(2,1)S(1)}, u32[]{:S(2)}, u32[]{:S(2)}) collective-permute-start(bf16[256,1280]{1,0:T(8,128)(2,1)S(1)} %pad_maximum_fusion.1.near_ref), channel_id=1, source_target_pairs={{0,4},{4,0},{8,12},{12,8},{1,5},{5,1},{9,13},{13,9},{2,6},{6,2},{1... | collective-permute-start | bytes 1966088 | tf_op jit(solution)/shard_map/ppermute | solution.py:255
  30.4 10.4 %collective-permute-start.3 = (bf16[128,1280]{1,0:T(8,128)(2,1)S(1)}, bf16[128,1280]{1,0:T(8,128)(2,1)S(1)}, u32[]{:S(2)}, u32[]{:S(2)}) collective-permute-start(bf16[128,1280]{1,0:T(8,128)(2,1)S(1)} %collective-permute-done.2), channel_id=1, source_target_pairs={{0,8},{4,12},{8,0},{12,4},{1,9},{5,13},{9,1},{13,5},{2,10},{6,14},... | collective-permute-start | bytes 983048 | tf_op jit(solution)/shard_map/ppermute | solution.py:244
  39.2 6.5 %collective-permute-start.8 = (bf16[256,1280]{1,0:T(8,128)(2,1)S(1)}, bf16[256,1280]{1,0:T(8,128)(2,1)S(1)}, u32[]{:S(2)}, u32[]{:S(2)}) collective-permute-start(bf16[256,1280]{1,0:T(8,128)(2,1)S(1)} %pad_maximum_fusion.near_ref), channel_id=1, source_target_pairs={{0,4},{4,0},{8,12},{12,8},{1,5},{5,1},{9,13},{13,9},{2,6},{6,2},{1... | collective-permute-start | bytes 1966088 | tf_op jit(solution)/shard_map/ppermute | solution.py:255
  40.8 10.2 %collective-permute-start.4 = (bf16[256,1280]{1,0:T(8,128)(2,1)S(1)}, bf16[256,1280]{1,0:T(8,128)(2,1)S(1)}, u32[]{:S(2)}, u32[]{:S(2)}) collective-permute-start(bf16[256,1280]{1,0:T(8,128)(2,1)S(1)} %constant_dynamic-update-slice_fusion.near_ref), channel_id=1, source_target_pairs={{0,4},{4,0},{8,12},{12,8},{1,5},{5,1},{9,13},{13,9},{2,6},{6,2},{1... | collective-permute-start | bytes 1966088 | tf_op jit(solution)/shard_map/ppermute | solution.py:255
  54.7 3.4 %collective-permute-start.13 = (bf16[256,1280]{1,0:T(8,128)(2,1)S(1)}, bf16[256,1280]{1,0:T(8,128)(2,1)S(1)}, u32[]{:S(2)}, u32[]{:S(2)}) collective-permute-start(bf16[256,1280]{1,0:T(8,128)(2,1)S(1)} %get-tuple-element.44), channel_id=1, source_target_pairs={{0,4},{4,0},{8,12},{12,8},{1,5},{5,1},{9,13},{13,9},{2,6},{6,2},{1... | collective-permute-start | bytes 1966088 | tf_op jit(solution)/shard_map/ppermute | solution.py:255
  57.9 4.4 %collective-permute-start.14 = (bf16[256,1280]{1,0:T(8,128)(2,1)S(1)}, bf16[256,1280]{1,0:T(8,128)(2,1)S(1)}, u32[]{:S(2)}, u32[]{:S(2)}) collective-permute-start(bf16[256,1280]{1,0:T(8,128)(2,1)S(1)} %get-tuple-element.47), channel_id=1, source_target_pairs={{0,4},{4,0},{8,12},{12,8},{1,5},{5,1},{9,13},{13,9},{2,6},{6,2},{1... | collective-permute-start | bytes 1966088 | tf_op jit(solution)/shard_map/ppermute | solution.py:255
  58.2 10.6 %collective-permute-start.18 = (bf16[128,1280]{1,0:T(8,128)(2,1)S(1)}, bf16[128,1280]{1,0:T(8,128)(2,1)S(1)}, u32[]{:S(2)}, u32[]{:S(2)}) collective-permute-start(bf16[128,1280]{1,0:T(8,128)(2,1)S(1)} %slice.67), channel_id=1, source_target_pairs={{0,8},{4,12},{8,0},{12,4},{1,9},{5,13},{9,1},{13,5},{2,10},{6,14},... | collective-permute-start | bytes 983048 | tf_op jit(solution)/shard_map/ppermute | solution.py:244
  62.5 12.9 %collective-permute-start.17 = (bf16[128,1280]{1,0:T(8,128)(2,1)S(1)}, bf16[128,1280]{1,0:T(8,128)(2,1)S(1)}, u32[]{:S(2)}, u32[]{:S(2)}) collective-permute-start(bf16[128,1280]{1,0:T(8,128)(2,1)S(1)} %slice.68), channel_id=1, source_target_pairs={{0,8},{4,12},{8,0},{12,4},{1,9},{5,13},{9,1},{13,5},{2,10},{6,14},... | collective-permute-start | bytes 983048 | tf_op jit(solution)/shard_map/ppermute | solution.py:244
  63.3 16.8 %collective-permute-start.21 = (bf16[256,1280]{1,0:T(8,128)(2,1)S(1)}, bf16[256,1280]{1,0:T(8,128)(2,1)S(1)}, u32[]{:S(2)}, u32[]{:S(2)}) collective-permute-start(bf16[256,1280]{1,0:T(8,128)(2,1)S(1)} %get-tuple-element.54), channel_id=1, source_target_pairs={{0,4},{4,0},{8,12},{12,8},{1,5},{5,1},{9,13},{13,9},{2,6},{6,2},{1... | collective-permute-start | bytes 1966088 | tf_op jit(solution)/shard_map/ppermute | solution.py:255
  68.8 9.5 %collective-permute-start.19 = (bf16[128,1280]{1,0:T(8,128)(2,1)S(1)}, bf16[128,1280]{1,0:T(8,128)(2,1)S(1)}, u32[]{:S(2)}, u32[]{:S(2)}) collective-permute-start(bf16[128,1280]{1,0:T(8,128)(2,1)S(1)} %add_convert_fusion.1), channel_id=1, source_target_pairs={{0,1},{1,0},{2,3},{3,2},{4,5},{5,4},{6,7},{7,6},{8,9},{9,8},{10,11... | collective-permute-start | bytes 983048 | tf_op jit(solution)/shard_map/ppermute | solution.py:239
  74.6 7.2 %collective-permute-start.15 = (bf16[256,1280]{1,0:T(8,128)(2,1)S(1)}, bf16[256,1280]{1,0:T(8,128)(2,1)S(1)}, u32[]{:S(2)}, u32[]{:S(2)}) collective-permute-start(bf16[256,1280]{1,0:T(8,128)(2,1)S(1)} %get-tuple-element.50), channel_id=1, source_target_pairs={{0,4},{4,0},{8,12},{12,8},{1,5},{5,1},{9,13},{13,9},{2,6},{6,2},{1... | collective-permute-start | bytes 1966088 | tf_op jit(solution)/shard_map/ppermute | solution.py:255
  78.4 15.6 %collective-permute-start.20 = (bf16[128,1280]{1,0:T(8,128)(2,1)S(1)}, bf16[128,1280]{1,0:T(8,128)(2,1)S(1)}, u32[]{:S(2)}, u32[]{:S(2)}) collective-permute-start(bf16[128,1280]{1,0:T(8,128)(2,1)S(1)} %add_convert_fusion), channel_id=1, source_target_pairs={{0,2},{1,3},{2,0},{3,1},{4,6},{5,7},{6,4},{7,5},{8,10},{9,11},{10,... | collective-permute-start | bytes 983048 | tf_op jit(solution)/shard_map/ppermute | solution.py:239
  80.3 10.5 %collective-permute-start.22 = (bf16[128,1280]{1,0:T(8,128)(2,1)S(1)}, bf16[128,1280]{1,0:T(8,128)(2,1)S(1)}, u32[]{:S(2)}, u32[]{:S(2)}) collective-permute-start(bf16[128,1280]{1,0:T(8,128)(2,1)S(1)} %slice.66), channel_id=1, source_target_pairs={{0,8},{4,12},{8,0},{12,4},{1,9},{5,13},{9,1},{13,5},{2,10},{6,14},... | collective-permute-start | bytes 983048 | tf_op jit(solution)/shard_map/ppermute | solution.py:244
  82.0 12.3 %collective-permute-start.16 = (bf16[128,1280]{1,0:T(8,128)(2,1)S(1)}, bf16[128,1280]{1,0:T(8,128)(2,1)S(1)}, u32[]{:S(2)}, u32[]{:S(2)}) collective-permute-start(bf16[128,1280]{1,0:T(8,128)(2,1)S(1)} %slice.69), channel_id=1, source_target_pairs={{0,8},{4,12},{8,0},{12,4},{1,9},{5,13},{9,1},{13,5},{2,10},{6,14},... | collective-permute-start | bytes 983048 | tf_op jit(solution)/shard_map/ppermute | solution.py:244
  90.9 9.2 %collective-permute-start.23 = (bf16[128,1280]{1,0:T(8,128)(2,1)S(1)}, bf16[128,1280]{1,0:T(8,128)(2,1)S(1)}, u32[]{:S(2)}, u32[]{:S(2)}) collective-permute-start(bf16[128,1280]{1,0:T(8,128)(2,1)S(1)} %fusion.4), channel_id=1, source_target_pairs={{0,1},{1,0},{2,3},{3,2},{4,5},{5,4},{6,7},{7,6},{8,9},{9,8},{10,11... | collective-permute-start | bytes 983048 | tf_op jit(solution)/shard_map/ppermute | solution.py:239

commit v4 on v3

--- a/solution.py
+++ b/solution.py
@@ -7,6 +7,7 @@
 from jax.experimental.pallas import tpu as pltpu
 from jax.sharding import PartitionSpec as P
 
+CUTS = 2
 VMEM_LIMIT = 20 * 1024 * 1024
 COST = 8000000000
 VMEM = pl.BlockSpec(memory_space=pltpu.VMEM)
@@ -42,18 +43,20 @@
 def load_parts(sources, part_refs, sems, block):
     local_count, _, width = sources[0].shape
     depth = part_refs[0].shape[1]
-    rows = pl.ds(pl.multiple_of(block * depth, depth), depth)
+    cut = depth // CUTS
     loads = []
     for index in range(local_count):
         copies = []
         for side, source in enumerate(sources):
-            if len(part_refs) == 1:
-                target = part_refs[0].at[index, :, side * width : (side + 1) * width]
-            else:
-                target = part_refs[side].at[index]
-            copies.append(
-                pltpu.make_async_copy(source.at[index, rows], target, sems.at[2 * index + side])
-            )
+            for k in range(CUTS):
+                rows = pl.ds(pl.multiple_of(block * depth + k * cut, cut), cut)
+                if len(part_refs) == 1:
+                    columns = slice(side * width, (side + 1) * width)
+                    target = part_refs[0].at[index, k * cut : (k + 1) * cut, columns]
+                else:
+                    target = part_refs[side].at[index, k * cut : (k + 1) * cut]
+                sem = sems.at[(2 * index + side) * CUTS + k]
+                copies.append(pltpu.make_async_copy(source.at[index, rows], target, sem))
         loads.append(copies)
     return loads
 
@@ -167,7 +170,7 @@
     first, loads_down = total is None, w_down is not None
     shapes = [jax.ShapeDtypeStruct((local_count, 2 * half, 2 * width), jnp.float32)]
     shapes += part_scratch(w_gate, depth)
-    scratch = [pltpu.SemaphoreType.DMA((2 * local_count,))]
+    scratch = [pltpu.SemaphoreType.DMA((2 * local_count * CUTS,))]
     if first:
         scratch = part_scratch(w_gate, depth) + scratch + scratch
     more, specs = [], []

time: 101 us -> 100 us (0.990)
  waiting for transfers between devices: 45.4 us -> 43.6 us
    ppermute x9, waiting for transfers between devices: 29.1 us -> 27.8 us  [over_chips(): lax.ppermute(value, 'expert', [(2 * i + c, 2 * ((i + shift) % chip_count)...]
  transfers between devices with their start and end apart: 24 -> 24, of which waited for: 13 -> 13; matrix products, arithmetic and copies ran while one was open for 5% -> 5% of each run, Pallas kernels for 23% -> 24%
where the time goes in v4:
time: 100 us
  waiting for transfers between devices  43.6 us (44%)
  Pallas kernels  27.4 us (27%)
  starting transfers between devices  23.3 us (23%)
  other arithmetic  4.11 us (4%)
  local copies, waits for them, and re-layouts  1.35 us (1%)
    ppermute x9, waiting for transfers between devices, over_chips(): lax.ppermute(value, 'expert', [(2 * i + c, 2 * ((i + shift) % chip_count)...  27.8 us
    ppermute x6, waiting for transfers between devices, over_seq(): return lax.ppermute(value, 'seq', [(i, i ^ flip) for i in range(seq_count)])  15.7 us
    pallas_call x3, Pallas kernels, gate_up(): call(functools.partial(gate_up_kernel, first, loads_down), shapes, [SMEM,...  15.7 us
    ppermute x6, starting transfers between devices, over_seq(): return lax.ppermute(value, 'seq', [(i, i ^ flip) for i in range(seq_count)])  12.4 us
    ppermute x9, starting transfers between devices, over_chips(): lax.ppermute(value, 'expert', [(2 * i + c, 2 * ((i + shift) % chip_count)...  9.88 us
    pallas_call x3, Pallas kernels, down(): call(down_kernel, down_shapes(value.shape[0] // 2, depth), [SMEM, VMEM, H...  8.13 us
    pallas_call x1, Pallas kernels, hidden(): call(hidden_kernel, [jax.ShapeDtypeStruct((row_count, local_count * width...  3.62 us
  transfers between devices with their start and end apart: 24, of which 13 were waited for; matrix products, arithmetic and copies ran while one was open for 5% of the time, Pallas kernels for 24%

profile of v4, /device:TPU:0, one launch (start us, length us, event | category | flops | bytes accessed | tf_op | source)
XLA Modules:
  0.0 100.1 jit_solution(6303237377573730475)
XLA Ops:
  0.0 3.0 %collective-permute-start = (bf16[128,1280]{1,0:T(8,128)(2,1)}, bf16[128,1280]{1,0:T(8,128)(2,1)S(1)}, u32[]{:S(2)}, u32[]{:S(2)}) collective-permute-start(bf16[128,1280]{1,0:T(8,128)(2,1)} %param.7), channel_id=1, source_target_pairs={{0,1},{1,0},{2,3},{3,2},{4,5},{5,4},{6,7},{7,6},{8,9},{9,8},{10,11... | collective-permute-start | bytes 983048 | tf_op jit(solution)/shard_map/ppermute | solution.py:242
  3.0 2.6 %collective-permute-start.1 = (bf16[128,1280]{1,0:T(8,128)(2,1)}, bf16[128,1280]{1,0:T(8,128)(2,1)S(1)}, u32[]{:S(2)}, u32[]{:S(2)}) collective-permute-start(bf16[128,1280]{1,0:T(8,128)(2,1)} %param.7), channel_id=1, source_target_pairs={{0,2},{1,3},{2,0},{3,1},{4,6},{5,7},{6,4},{7,5},{8,10},{9,11},{10,... | collective-permute-start | bytes 983048 | tf_op jit(solution)/shard_map/ppermute | solution.py:242
  5.6 1.5 %collective-permute-start.6 = (bf16[128,1280]{1,0:T(8,128)(2,1)}, bf16[128,1280]{1,0:T(8,128)(2,1)S(1)}, u32[]{:S(2)}, u32[]{:S(2)}) collective-permute-start(bf16[128,1280]{1,0:T(8,128)(2,1)} %param.7), channel_id=1, source_target_pairs={{0,8},{4,12},{8,0},{12,4},{1,9},{5,13},{9,1},{13,5},{2,10},{6,14},... | collective-permute-start | bytes 983048 | tf_op jit(solution)/shard_map/ppermute | solution.py:247
  11.1 3.7 %collective-permute-done.10 = f32[1,8,128]{2,1,0:T(8,128)S(1)} collective-permute-done((f32[1,8,128]{2,1,0:T(8,128)S(1)}, f32[1,8,128]{2,1,0:T(8,128)S(1)}, u32[]{:S(2)}, u32[]{:S(2)}) %collective-permute-start.10) | collective-permute-done | bytes 4128 | tf_op jit(solution)/shard_map/ppermute | solution.py:247
  14.9 2.9 %collective-permute-done = bf16[128,1280]{1,0:T(8,128)(2,1)S(1)} collective-permute-done((bf16[128,1280]{1,0:T(8,128)(2,1)}, bf16[128,1280]{1,0:T(8,128)(2,1)S(1)}, u32[]{:S(2)}, u32[]{:S(2)}) %collective-permute-start) | collective-permute-done | bytes 327712 | tf_op jit(solution)/shard_map/ppermute | solution.py:242
  17.8 2.6 %collective-permute-done.1 = bf16[128,1280]{1,0:T(8,128)(2,1)S(1)} collective-permute-done((bf16[128,1280]{1,0:T(8,128)(2,1)}, bf16[128,1280]{1,0:T(8,128)(2,1)S(1)}, u32[]{:S(2)}, u32[]{:S(2)}) %collective-permute-start.1) | collective-permute-done | bytes 327712 | tf_op jit(solution)/shard_map/ppermute | solution.py:242
  20.4 1.5 %collective-permute-start.9 = (bf16[128,1280]{1,0:T(8,128)(2,1)S(1)}, bf16[128,1280]{1,0:T(8,128)(2,1)S(1)}, u32[]{:S(2)}, u32[]{:S(2)}) collective-permute-start(bf16[128,1280]{1,0:T(8,128)(2,1)S(1)} %collective-permute-done), channel_id=1, source_target_pairs={{0,8},{4,12},{8,0},{12,4},{1,9},{5,13},{9,1},{13,5},{2,10},{6,14},... | collective-permute-start | bytes 983048 | tf_op jit(solution)/shard_map/ppermute | solution.py:247
  23.2 7.1 %collective-permute-done.9 = bf16[128,1280]{1,0:T(8,128)(2,1)S(1)} collective-permute-done((bf16[128,1280]{1,0:T(8,128)(2,1)S(1)}, bf16[128,1280]{1,0:T(8,128)(2,1)S(1)}, u32[]{:S(2)}, u32[]{:S(2)}) %collective-permute-start.9) | collective-permute-done | bytes 327712 | tf_op jit(solution)/shard_map/ppermute | solution.py:247
  31.8 2.2 %collective-permute-done.5 = bf16[128,1280]{1,0:T(8,128)(2,1)S(1)} collective-permute-done((bf16[128,1280]{1,0:T(8,128)(2,1)S(1)}, bf16[128,1280]{1,0:T(8,128)(2,1)S(1)}, u32[]{:S(2)}, u32[]{:S(2)}) %collective-permute-start.5) | collective-permute-done | bytes 327712 | tf_op jit(solution)/shard_map/ppermute | solution.py:247
  34.0 5.6 %shard_map.73 = (f32[2,512,768]{2,1,0:T(8,128)S(1)}, bf16[2,1280,768]{2,1,0:T(8,128)(2,1)S(1)}) custom-call(s32[2]{0:T(128)S(1)} %pad_add_fusion.1.at_ref, bf16[256,1280]{1,0:T(8,128)(2,1)S(1)} %constant_dynamic-update-slice_fusion.2.near_ref, bf16[256,1280]{1,0:T(8,128)(2,1)S(1)} %collective-permute-done.7.far_ref, bf16[2,5120,384]{2,1,0:T(8,128)(2,1)} %gate_ref.5, ...), custom_call_target="tpu_custom_call" | custom-call | flops 8000000000 | bytes 8000000000 | tf_op jit(solution)/shard_map/pallas_call | solution.py:185
  40.9 4.6 %shard_map.74 = (f32[2,512,768]{2,1,0:T(8,128)S(1)}, bf16[2,1280,768]{2,1,0:T(8,128)(2,1)S(1)}) custom-call(s32[2]{0:T(128)S(1)} %pad_add_fusion.2.at_ref, bf16[256,1280]{1,0:T(8,128)(2,1)S(1)} %pad_maximum_fusion.1.near_ref, bf16[256,1280]{1,0:T(8,128)(2,1)S(1)} %collective-permute-done.12.far_ref, bf16[2,5120,384]{2,1,0:T(8,128)(2,1)} %gate_ref.5, ...), custom_call_target="tpu_custom_call" | custom-call | flops 8000000000 | bytes 8000000000 | tf_op jit(solution)/shard_map/pallas_call | solution.py:185
  45.6 5.4 %shard_map.75 = (f32[2,512,768]{2,1,0:T(8,128)S(1)}, bf16[2,1280,768]{2,1,0:T(8,128)(2,1)S(1)}, bf16[2,384,1280]{2,1,0:T(8,128)(2,1)S(1)}) custom-call(s32[2]{0:T(128)S(1)} %pad_add_fusion.at_ref, bf16[256,1280]{1,0:T(8,128)(2,1)S(1)} %pad_maximum_fusion.near_ref, bf16[256,1280]{1,0:T(8,128)(2,1)S(1)} %collective-permute-done.8.far_ref, ...), custom_call_target="tpu_custom_call" | custom-call | flops 8000000000 | bytes 8000000000 | tf_op jit(solution)/shard_map/pallas_call | solution.py:185
  51.0 3.6 %shard_map.76 = (bf16[512,768]{1,0:T(8,128)(2,1)S(1)}, f32[256,1280]{1,0:T(8,128)S(1)}, bf16[256,1280]{1,0:T(8,128)(2,1)S(1)}) custom-call(bf16[256,1280]{1,0:T(8,128)(2,1)S(1)} %constant_dynamic-update-slice_fusion.near_ref, bf16[256,1280]{1,0:T(8,128)(2,1)S(1)} %collective-permute-done.4.far_ref, f32[2,512,768]{2,1,0:T(8,128)S(1)} %get-tuple-element.38.total_ref, ...), custom_call_target="tpu_custom_call" | custom-call | flops 8000000000 | bytes 8000000000 | tf_op jit(solution)/shard_map/pallas_call | solution.py:197
  55.2 2.7 %shard_map.77 = (f32[256,1280]{1,0:T(8,128)S(1)}, bf16[256,1280]{1,0:T(8,128)(2,1)S(1)}) custom-call(s32[1]{0:T(128)} %bitcast.1.at_ref, bf16[512,768]{1,0:T(8,128)(2,1)S(1)} %get-tuple-element.48.hidden_ref, bf16[2,384,5120]{2,1,0:T(8,128)(2,1)} %down_ref.5), custom_call_target="tpu_custom_call" | custom-call | flops 8000000000 | bytes 8000000000 | tf_op jit(solution)/shard_map/pallas_call | solution.py:206
  59.6 2.7 %shard_map.79 = (f32[256,1280]{1,0:T(8,128)S(1)}, bf16[256,1280]{1,0:T(8,128)(2,1)S(1)}) custom-call(s32[1]{0:T(128)} %bitcast.3.at_ref, bf16[512,768]{1,0:T(8,128)(2,1)S(1)} %get-tuple-element.48.hidden_ref, bf16[2,384,5120]{2,1,0:T(8,128)(2,1)} %down_ref.5), custom_call_target="tpu_custom_call" | custom-call | flops 8000000000 | bytes 8000000000 | tf_op jit(solution)/shard_map/pallas_call | solution.py:206
  63.2 5.5 %collective-permute-done.18 = bf16[128,1280]{1,0:T(8,128)(2,1)S(1)} collective-permute-done((bf16[128,1280]{1,0:T(8,128)(2,1)S(1)}, bf16[128,1280]{1,0:T(8,128)(2,1)S(1)}, u32[]{:S(2)}, u32[]{:S(2)}) %collective-permute-start.18) | collective-permute-done | bytes 327712 | tf_op jit(solution)/shard_map/ppermute | solution.py:247
  68.8 3.6 %collective-permute-start.19 = (bf16[128,1280]{1,0:T(8,128)(2,1)S(1)}, bf16[128,1280]{1,0:T(8,128)(2,1)S(1)}, u32[]{:S(2)}, u32[]{:S(2)}) collective-permute-start(bf16[128,1280]{1,0:T(8,128)(2,1)S(1)} %add_convert_fusion.1), channel_id=1, source_target_pairs={{0,1},{1,0},{2,3},{3,2},{4,5},{5,4},{6,7},{7,6},{8,9},{9,8},{10,11... | collective-permute-start | bytes 983048 | tf_op jit(solution)/shard_map/ppermute | solution.py:242
  72.4 2.7 %shard_map.78 = (f32[256,1280]{1,0:T(8,128)S(1)}, bf16[256,1280]{1,0:T(8,128)(2,1)S(1)}) custom-call(s32[1]{0:T(128)} %bitcast.at_ref, bf16[512,768]{1,0:T(8,128)(2,1)S(1)} %get-tuple-element.48.hidden_ref, bf16[2,384,5120]{2,1,0:T(8,128)(2,1)} %down_ref.5), custom_call_target="tpu_custom_call" | custom-call | flops 8000000000 | bytes 8000000000 | tf_op jit(solution)/shard_map/pallas_call | solution.py:206
  75.3 3.1 %collective-permute-done.19 = bf16[128,1280]{1,0:T(8,128)(2,1)S(1)} collective-permute-done((bf16[128,1280]{1,0:T(8,128)(2,1)S(1)}, bf16[128,1280]{1,0:T(8,128)(2,1)S(1)}, u32[]{:S(2)}, u32[]{:S(2)}) %collective-permute-start.19) | collective-permute-done | bytes 327712 | tf_op jit(solution)/shard_map/ppermute | solution.py:242
  78.6 1.7 %collective-permute-start.20 = (bf16[128,1280]{1,0:T(8,128)(2,1)S(1)}, bf16[128,1280]{1,0:T(8,128)(2,1)S(1)}, u32[]{:S(2)}, u32[]{:S(2)}) collective-permute-start(bf16[128,1280]{1,0:T(8,128)(2,1)S(1)} %add_convert_fusion), channel_id=1, source_target_pairs={{0,2},{1,3},{2,0},{3,1},{4,6},{5,7},{6,4},{7,5},{8,10},{9,11},{10,... | collective-permute-start | bytes 983048 | tf_op jit(solution)/shard_map/ppermute | solution.py:242
  80.5 1.6 %collective-permute-start.22 = (bf16[128,1280]{1,0:T(8,128)(2,1)S(1)}, bf16[128,1280]{1,0:T(8,128)(2,1)S(1)}, u32[]{:S(2)}, u32[]{:S(2)}) collective-permute-start(bf16[128,1280]{1,0:T(8,128)(2,1)S(1)} %slice.66), channel_id=1, source_target_pairs={{0,8},{4,12},{8,0},{12,4},{1,9},{5,13},{9,1},{13,5},{2,10},{6,14},... | collective-permute-start | bytes 983048 | tf_op jit(solution)/shard_map/ppermute | solution.py:247
  82.8 7.9 %collective-permute-done.22 = bf16[128,1280]{1,0:T(8,128)(2,1)S(1)} collective-permute-done((bf16[128,1280]{1,0:T(8,128)(2,1)S(1)}, bf16[128,1280]{1,0:T(8,128)(2,1)S(1)}, u32[]{:S(2)}, u32[]{:S(2)}) %collective-permute-start.22) | collective-permute-done | bytes 327712 | tf_op jit(solution)/shard_map/ppermute | solution.py:247
  91.9 2.0 %collective-permute-done.20 = bf16[128,1280]{1,0:T(8,128)(2,1)S(1)} collective-permute-done((bf16[128,1280]{1,0:T(8,128)(2,1)S(1)}, bf16[128,1280]{1,0:T(8,128)(2,1)S(1)}, u32[]{:S(2)}, u32[]{:S(2)}) %collective-permute-start.20) | collective-permute-done | bytes 327712 | tf_op jit(solution)/shard_map/ppermute | solution.py:242
  94.2 5.0 %collective-permute-done.23 = bf16[128,1280]{1,0:T(8,128)(2,1)S(1)} collective-permute-done((bf16[128,1280]{1,0:T(8,128)(2,1)S(1)}, bf16[128,1280]{1,0:T(8,128)(2,1)S(1)}, u32[]{:S(2)}, u32[]{:S(2)}) %collective-permute-start.23) | collective-permute-done | bytes 327712 | tf_op jit(solution)/shard_map/ppermute | solution.py:242
  (59 shorter events, 15.0 us)
Async XLA Ops:
  0.0 17.8 %collective-permute-start = (bf16[128,1280]{1,0:T(8,128)(2,1)}, bf16[128,1280]{1,0:T(8,128)(2,1)S(1)}, u32[]{:S(2)}, u32[]{:S(2)}) collective-permute-start(bf16[128,1280]{1,0:T(8,128)(2,1)} %param.7), channel_id=1, source_target_pairs={{0,1},{1,0},{2,3},{3,2},{4,5},{5,4},{6,7},{7,6},{8,9},{9,8},{10,11... | collective-permute-start | bytes 983048 | tf_op jit(solution)/shard_map/ppermute | solution.py:242
  3.0 17.4 %collective-permute-start.1 = (bf16[128,1280]{1,0:T(8,128)(2,1)}, bf16[128,1280]{1,0:T(8,128)(2,1)S(1)}, u32[]{:S(2)}, u32[]{:S(2)}) collective-permute-start(bf16[128,1280]{1,0:T(8,128)(2,1)} %param.7), channel_id=1, source_target_pairs={{0,2},{1,3},{2,0},{3,1},{4,6},{5,7},{6,4},{7,5},{8,10},{9,11},{10,... | collective-permute-start | bytes 983048 | tf_op jit(solution)/shard_map/ppermute | solution.py:242
  5.6 17.5 %collective-permute-start.6 = (bf16[128,1280]{1,0:T(8,128)(2,1)}, bf16[128,1280]{1,0:T(8,128)(2,1)S(1)}, u32[]{:S(2)}, u32[]{:S(2)}) collective-permute-start(bf16[128,1280]{1,0:T(8,128)(2,1)} %param.7), channel_id=1, source_target_pairs={{0,8},{4,12},{8,0},{12,4},{1,9},{5,13},{9,1},{13,5},{2,10},{6,14},... | collective-permute-start | bytes 983048 | tf_op jit(solution)/shard_map/ppermute | solution.py:247
  9.4 5.4 %collective-permute-start.10 = (f32[1,8,128]{2,1,0:T(8,128)S(1)}, f32[1,8,128]{2,1,0:T(8,128)S(1)}, u32[]{:S(2)}, u32[]{:S(2)}) collective-permute-start(f32[1,8,128]{2,1,0:T(8,128)S(1)} %fusion.3), channel_id=1, source_target_pairs={{0,8},{4,12},{8,0},{12,4},{1,9},{5,13},{9,1},{13,5},{2,10},{6,14},... | collective-permute-start | bytes 12296 | tf_op jit(solution)/shard_map/ppermute | solution.py:247
  14.8 7.1 %collective-permute-start.11 = (f32[2,8,128]{2,1,0:T(8,128)S(1)}, f32[2,8,128]{2,1,0:T(8,128)S(1)}, u32[]{:S(2)}, u32[]{:S(2)}) collective-permute-start(f32[2,8,128]{2,1,0:T(8,128)S(1)} %pad_maximum_fusion.2), channel_id=1, source_target_pairs={{0,4},{4,0},{8,12},{12,8},{1,5},{5,1},{9,13},{13,9},{2,6},{6,2},{1... | collective-permute-start | bytes 24584 | tf_op jit(solution)/shard_map/ppermute | solution.py:258
  20.4 9.9 %collective-permute-start.9 = (bf16[128,1280]{1,0:T(8,128)(2,1)S(1)}, bf16[128,1280]{1,0:T(8,128)(2,1)S(1)}, u32[]{:S(2)}, u32[]{:S(2)}) collective-permute-start(bf16[128,1280]{1,0:T(8,128)(2,1)S(1)} %collective-permute-done), channel_id=1, source_target_pairs={{0,8},{4,12},{8,0},{12,4},{1,9},{5,13},{9,1},{13,5},{2,10},{6,14},... | collective-permute-start | bytes 983048 | tf_op jit(solution)/shard_map/ppermute | solution.py:247
  22.0 11.9 %collective-permute-start.5 = (bf16[128,1280]{1,0:T(8,128)(2,1)S(1)}, bf16[128,1280]{1,0:T(8,128)(2,1)S(1)}, u32[]{:S(2)}, u32[]{:S(2)}) collective-permute-start(bf16[128,1280]{1,0:T(8,128)(2,1)S(1)} %collective-permute-done.1), channel_id=1, source_target_pairs={{0,8},{4,12},{8,0},{12,4},{1,9},{5,13},{9,1},{13,5},{2,10},{6,14},... | collective-permute-start | bytes 983048 | tf_op jit(solution)/shard_map/ppermute | solution.py:247
  22.6 7.7 %collective-permute-start.2 = (bf16[128,1280]{1,0:T(8,128)(2,1)S(1)}, bf16[128,1280]{1,0:T(8,128)(2,1)S(1)}, u32[]{:S(2)}, u32[]{:S(2)}) collective-permute-start(bf16[128,1280]{1,0:T(8,128)(2,1)S(1)} %collective-permute-done.1), channel_id=1, source_target_pairs={{0,1},{1,0},{2,3},{3,2},{4,5},{5,4},{6,7},{7,6},{8,9},{9,8},{10,11... | collective-permute-start | bytes 983048 | tf_op jit(solution)/shard_map/ppermute | solution.py:242
  23.1 10.9 %collective-permute-start.7 = (bf16[256,1280]{1,0:T(8,128)(2,1)S(1)}, bf16[256,1280]{1,0:T(8,128)(2,1)S(1)}, u32[]{:S(2)}, u32[]{:S(2)}) collective-permute-start(bf16[256,1280]{1,0:T(8,128)(2,1)S(1)} %constant_dynamic-update-slice_fusion.2.near_ref), channel_id=1, source_target_pairs={{0,4},{4,0},{8,12},{12,8},{1,5},{5,1},{9,13},{13,9},{2,6},{6,2},{1... | collective-permute-start | bytes 1966088 | tf_op jit(solution)/shard_map/ppermute | solution.py:258
  30.3 10.6 %collective-permute-start.12 = (bf16[256,1280]{1,0:T(8,128)(2,1)S(1)}, bf16[256,1280]{1,0:T(8,128)(2,1)S(1)}, u32[]{:S(2)}, u32[]{:S(2)}) collective-permute-start(bf16[256,1280]{1,0:T(8,128)(2,1)S(1)} %pad_maximum_fusion.1.near_ref), channel_id=1, source_target_pairs={{0,4},{4,0},{8,12},{12,8},{1,5},{5,1},{9,13},{13,9},{2,6},{6,2},{1... | collective-permute-start | bytes 1966088 | tf_op jit(solution)/shard_map/ppermute | solution.py:258
  30.4 10.4 %collective-permute-start.3 = (bf16[128,1280]{1,0:T(8,128)(2,1)S(1)}, bf16[128,1280]{1,0:T(8,128)(2,1)S(1)}, u32[]{:S(2)}, u32[]{:S(2)}) collective-permute-start(bf16[128,1280]{1,0:T(8,128)(2,1)S(1)} %collective-permute-done.2), channel_id=1, source_target_pairs={{0,8},{4,12},{8,0},{12,4},{1,9},{5,13},{9,1},{13,5},{2,10},{6,14},... | collective-permute-start | bytes 983048 | tf_op jit(solution)/shard_map/ppermute | solution.py:247
  39.7 5.9 %collective-permute-start.8 = (bf16[256,1280]{1,0:T(8,128)(2,1)S(1)}, bf16[256,1280]{1,0:T(8,128)(2,1)S(1)}, u32[]{:S(2)}, u32[]{:S(2)}) collective-permute-start(bf16[256,1280]{1,0:T(8,128)(2,1)S(1)} %pad_maximum_fusion.near_ref), channel_id=1, source_target_pairs={{0,4},{4,0},{8,12},{12,8},{1,5},{5,1},{9,13},{13,9},{2,6},{6,2},{1... | collective-permute-start | bytes 1966088 | tf_op jit(solution)/shard_map/ppermute | solution.py:258
  40.8 10.2 %collective-permute-start.4 = (bf16[256,1280]{1,0:T(8,128)(2,1)S(1)}, bf16[256,1280]{1,0:T(8,128)(2,1)S(1)}, u32[]{:S(2)}, u32[]{:S(2)}) collective-permute-start(bf16[256,1280]{1,0:T(8,128)(2,1)S(1)} %constant_dynamic-update-slice_fusion.near_ref), channel_id=1, source_target_pairs={{0,4},{4,0},{8,12},{12,8},{1,5},{5,1},{9,13},{13,9},{2,6},{6,2},{1... | collective-permute-start | bytes 1966088 | tf_op jit(solution)/shard_map/ppermute | solution.py:258
  54.6 3.4 %collective-permute-start.13 = (bf16[256,1280]{1,0:T(8,128)(2,1)S(1)}, bf16[256,1280]{1,0:T(8,128)(2,1)S(1)}, u32[]{:S(2)}, u32[]{:S(2)}) collective-permute-start(bf16[256,1280]{1,0:T(8,128)(2,1)S(1)} %get-tuple-element.44), channel_id=1, source_target_pairs={{0,4},{4,0},{8,12},{12,8},{1,5},{5,1},{9,13},{13,9},{2,6},{6,2},{1... | collective-permute-start | bytes 1966088 | tf_op jit(solution)/shard_map/ppermute | solution.py:258
  57.9 4.4 %collective-permute-start.14 = (bf16[256,1280]{1,0:T(8,128)(2,1)S(1)}, bf16[256,1280]{1,0:T(8,128)(2,1)S(1)}, u32[]{:S(2)}, u32[]{:S(2)}) collective-permute-start(bf16[256,1280]{1,0:T(8,128)(2,1)S(1)} %get-tuple-element.47), channel_id=1, source_target_pairs={{0,4},{4,0},{8,12},{12,8},{1,5},{5,1},{9,13},{13,9},{2,6},{6,2},{1... | collective-permute-start | bytes 1966088 | tf_op jit(solution)/shard_map/ppermute | solution.py:258
  58.2 10.6 %collective-permute-start.18 = (bf16[128,1280]{1,0:T(8,128)(2,1)S(1)}, bf16[128,1280]{1,0:T(8,128)(2,1)S(1)}, u32[]{:S(2)}, u32[]{:S(2)}) collective-permute-start(bf16[128,1280]{1,0:T(8,128)(2,1)S(1)} %slice.67), channel_id=1, source_target_pairs={{0,8},{4,12},{8,0},{12,4},{1,9},{5,13},{9,1},{13,5},{2,10},{6,14},... | collective-permute-start | bytes 983048 | tf_op jit(solution)/shard_map/ppermute | solution.py:247
  62.5 12.9 %collective-permute-start.17 = (bf16[128,1280]{1,0:T(8,128)(2,1)S(1)}, bf16[128,1280]{1,0:T(8,128)(2,1)S(1)}, u32[]{:S(2)}, u32[]{:S(2)}) collective-permute-start(bf16[128,1280]{1,0:T(8,128)(2,1)S(1)} %slice.68), channel_id=1, source_target_pairs={{0,8},{4,12},{8,0},{12,4},{1,9},{5,13},{9,1},{13,5},{2,10},{6,14},... | collective-permute-start | bytes 983048 | tf_op jit(solution)/shard_map/ppermute | solution.py:247
  63.2 17.1 %collective-permute-start.21 = (bf16[256,1280]{1,0:T(8,128)(2,1)S(1)}, bf16[256,1280]{1,0:T(8,128)(2,1)S(1)}, u32[]{:S(2)}, u32[]{:S(2)}) collective-permute-start(bf16[256,1280]{1,0:T(8,128)(2,1)S(1)} %get-tuple-element.54), channel_id=1, source_target_pairs={{0,4},{4,0},{8,12},{12,8},{1,5},{5,1},{9,13},{13,9},{2,6},{6,2},{1... | collective-permute-start | bytes 1966088 | tf_op jit(solution)/shard_map/ppermute | solution.py:258
  68.8 9.7 %collective-permute-start.19 = (bf16[128,1280]{1,0:T(8,128)(2,1)S(1)}, bf16[128,1280]{1,0:T(8,128)(2,1)S(1)}, u32[]{:S(2)}, u32[]{:S(2)}) collective-permute-start(bf16[128,1280]{1,0:T(8,128)(2,1)S(1)} %add_convert_fusion.1), channel_id=1, source_target_pairs={{0,1},{1,0},{2,3},{3,2},{4,5},{5,4},{6,7},{7,6},{8,9},{9,8},{10,11... | collective-permute-start | bytes 983048 | tf_op jit(solution)/shard_map/ppermute | solution.py:242
  75.1 6.9 %collective-permute-start.15 = (bf16[256,1280]{1,0:T(8,128)(2,1)S(1)}, bf16[256,1280]{1,0:T(8,128)(2,1)S(1)}, u32[]{:S(2)}, u32[]{:S(2)}) collective-permute-start(bf16[256,1280]{1,0:T(8,128)(2,1)S(1)} %get-tuple-element.50), channel_id=1, source_target_pairs={{0,4},{4,0},{8,12},{12,8},{1,5},{5,1},{9,13},{13,9},{2,6},{6,2},{1... | collective-permute-start | bytes 1966088 | tf_op jit(solution)/shard_map/ppermute | solution.py:258
  78.6 15.3 %collective-permute-start.20 = (bf16[128,1280]{1,0:T(8,128)(2,1)S(1)}, bf16[128,1280]{1,0:T(8,128)(2,1)S(1)}, u32[]{:S(2)}, u32[]{:S(2)}) collective-permute-start(bf16[128,1280]{1,0:T(8,128)(2,1)S(1)} %add_convert_fusion), channel_id=1, source_target_pairs={{0,2},{1,3},{2,0},{3,1},{4,6},{5,7},{6,4},{7,5},{8,10},{9,11},{10,... | collective-permute-start | bytes 983048 | tf_op jit(solution)/shard_map/ppermute | solution.py:242
  80.5 10.2 %collective-permute-start.22 = (bf16[128,1280]{1,0:T(8,128)(2,1)S(1)}, bf16[128,1280]{1,0:T(8,128)(2,1)S(1)}, u32[]{:S(2)}, u32[]{:S(2)}) collective-permute-start(bf16[128,1280]{1,0:T(8,128)(2,1)S(1)} %slice.66), channel_id=1, source_target_pairs={{0,8},{4,12},{8,0},{12,4},{1,9},{5,13},{9,1},{13,5},{2,10},{6,14},... | collective-permute-start | bytes 983048 | tf_op jit(solution)/shard_map/ppermute | solution.py:247
  82.2 12.0 %collective-permute-start.16 = (bf16[128,1280]{1,0:T(8,128)(2,1)S(1)}, bf16[128,1280]{1,0:T(8,128)(2,1)S(1)}, u32[]{:S(2)}, u32[]{:S(2)}) collective-permute-start(bf16[128,1280]{1,0:T(8,128)(2,1)S(1)} %slice.69), channel_id=1, source_target_pairs={{0,8},{4,12},{8,0},{12,4},{1,9},{5,13},{9,1},{13,5},{2,10},{6,14},... | collective-permute-start | bytes 983048 | tf_op jit(solution)/shard_map/ppermute | solution.py:247
  90.8 8.5 %collective-permute-start.23 = (bf16[128,1280]{1,0:T(8,128)(2,1)S(1)}, bf16[128,1280]{1,0:T(8,128)(2,1)S(1)}, u32[]{:S(2)}, u32[]{:S(2)}) collective-permute-start(bf16[128,1280]{1,0:T(8,128)(2,1)S(1)} %fusion.4), channel_id=1, source_target_pairs={{0,1},{1,0},{2,3},{3,2},{4,5},{5,4},{6,7},{7,6},{8,9},{9,8},{10,11... | collective-permute-start | bytes 983048 | tf_op jit(solution)/shard_map/ppermute | solution.py:242
